TPU v7x, 32 devices: a whole 2x2x4 slice. The times are simulated.
32 devices in a mesh: seq: 16 (over z, y, x), head: 2 (over core).
Axes of the slice: x: 2, y: 2, z: 4, core: 2. Of those that a mesh axis runs over, the one named last changes fastest.
Arguments:
- hidden_in: bfloat16 [1024, 2, 1536], P('seq'), may hold values from -4 to 4
- doc_ids: int32 [1024, 2], P('seq'), may hold values from 0 to 3, as said below
- routes: int32 [1024, 2, 6], P('seq'), may hold values from 0 to 15, all different within a row; in each aligned block of 128 rows (0 to 127, 128 to 255, ..., all dimensions but the last counted through in order) at most 96 rows name the same one
- norm1_gain: float32 [1536], replicated, may hold values from 0.5 to 1.5
- w_z: bfloat16 [1536, 3072], P('seq', 'head'), may hold values from -4 to 4
- w_x: bfloat16 [1536, 3072], P('seq', 'head'), may hold values from -4 to 4
- w_bc: bfloat16 [1536, 256], P('seq'), may hold values from -4 to 4
- w_dt: bfloat16 [1536, 48], P('seq', 'head'), may hold values from -4 to 4
- conv_x: float32 [4, 3072], P(None, 'head'), may hold values from -4 to 4
- conv_bc: float32 [4, 256], replicated, may hold values from -4 to 4
- convb_x: float32 [3072], P('head'), may hold values from -4 to 4
- convb_bc: float32 [256], replicated, may hold values from -4 to 4
- dt_bias: float32 [48], P('head'), may hold values from -1 to 1
- a_log: float32 [48], P('head'), may hold values from -10 to -3.5
- d_skip: float32 [48], P('head'), may hold values from 0.5 to 2
- gnorm_gain: float32 [3072], P('head'), may hold values from 0.5 to 1.5
- w_out: bfloat16 [3072, 1536], P('head', 'seq'), may hold values from -4 to 4
- norm2_gain: float32 [1536], replicated, may hold values from 0.5 to 1.5
- router: bfloat16 [1536, 16], P('seq'), may hold values from -4 to 4
- shared_gate: bfloat16 [1536, 1024], P('seq', 'head'), may hold values from -4 to 4
- shared_up: bfloat16 [1536, 1024], P('seq', 'head'), may hold values from -4 to 4
- shared_down: bfloat16 [1024, 1536], P('head', 'seq'), may hold values from -4 to 4
- expert_gate: bfloat16 [16, 1536, 512], P('seq', None, 'head'), may hold values from -4 to 4
- expert_up: bfloat16 [16, 1536, 512], P('seq', None, 'head'), may hold values from -4 to 4
- expert_down: bfloat16 [16, 512, 1536], P('seq', 'head'), may hold values from -4 to 4
- cotangent: bfloat16 [1024, 2, 1536], P('seq'), may hold values from -4 to 4
Outputs:
- block_out: float32 [1024, 2, 1536], P('seq')
- input_grad: float32 [1024, 2, 1536], P('seq')
- norm1_gain_grad: float32 [1536], replicated
- w_z_grad: float32 [1536, 3072], P('seq', 'head')
- w_x_grad: float32 [1536, 3072], P('seq', 'head')
- w_bc_grad: float32 [1536, 256], P('seq')
- w_dt_grad: float32 [1536, 48], P('seq', 'head')
- conv_x_grad: float32 [4, 3072], P(None, 'head')
- conv_bc_grad: float32 [4, 256], replicated
- convb_x_grad: float32 [3072], P('head')
- convb_bc_grad: float32 [256], replicated
- dt_bias_grad: float32 [48], P('head')
- a_log_grad: float32 [48], P('head')
- d_skip_grad: float32 [48], P('head')
- gnorm_gain_grad: float32 [3072], P('head')
- w_out_grad: float32 [3072, 1536], P('head', 'seq')
- norm2_gain_grad: float32 [1536], replicated
- router_grad: float32 [1536, 16], P('seq')
- shared_gate_grad: float32 [1536, 1024], P('seq', 'head')
- shared_up_grad: float32 [1536, 1024], P('seq', 'head')
- shared_down_grad: float32 [1024, 1536], P('head', 'seq')
- expert_gate_grad: float32 [16, 1536, 512], P('seq', None, 'head')
- expert_up_grad: float32 [16, 1536, 512], P('seq', None, 'head')
- expert_down_grad: float32 [16, 512, 1536], P('seq', 'head')
Inputs may be any that keep to these rules, and one draw needn't show every extreme that they name: `doc_ids`: document numbers along each sequence start at 0 and rise by one at the first position of each document. One sequence, drawn from the seed, is a single document; every other one holds 4 documents. `routes`: each token names 6 different experts. Among the 128 tokens of one index of seq (position-major storage order) no expert is named by more than 96 tokens, a bound that some block reaches.
All inputs are finite; a program needn't handle non-finite values.
Results may differ from a plain program's by a relative error of at most 0.024.
The roundings to bfloat16 on the way count: a program that leaves them out, or rounds other values in their place, can miss the bound.
Values may be sent and summed in bfloat16 or wider, within the bound.
A program may use at most 384 MiB of HBM per device.

v0:
```python
import jax
import jax.numpy as jnp
from jax import lax
from jax.sharding import PartitionSpec as P

KER = 4
INNER = 3072


EPS = 1e-05
HIGH = lax.Precision.HIGHEST


def passed_along(array, axis, by):
    length = lax.axis_size(axis)
    pairs = [(i, i + by) for i in range(length) if 0 <= i + by < length]
    return lax.ppermute(array, axis, pairs)


def entering(array, axis, combine, identity, reverse):
    length, here = (lax.axis_size(axis), lax.axis_index(axis))
    everything = jax.tree.map(
        lambda part, kind: lax.all_gather(part.astype(kind), axis),
        array,
        jax.tree.map(lambda a: jnp.bfloat16 if a.dtype == jnp.float32 else a.dtype, array),
    )
    start = jax.tree.map(
        lambda part, zero: jnp.broadcast_to(jnp.asarray(zero, part.dtype), part.shape),
        array,
        identity,
    )

    def hop(k, before):
        at = length - 1 - k if reverse else k
        reached = at > here if reverse else at < here
        new = combine(
            before, jax.tree.map(lambda part, own: part[at].astype(own.dtype), everything, array)
        )
        return jax.tree.map(lambda a, b: jnp.where(reached, a, b), new, before)

    return lax.fori_loop(0, length, hop, start)


def shortened(array):

    def short(part):
        return part.astype(jnp.bfloat16) if part.dtype == jnp.float32 else part

    return jax.tree.map(short, array)


def conv_apply(conv_ext, docs_ext, weight, conv_bias):
    length_here = conv_ext.shape[0] - (KER - 1)
    running = conv_bias
    for offset in range(KER):
        same_doc = (docs_ext[offset : offset + length_here] == docs_ext[KER - 1 :]).astype(
            jnp.float32
        )
        running = (
            running + weight[offset] * conv_ext[offset : offset + length_here] * same_doc[..., None]
        )
    return jax.nn.silu(running)


def group_parts(x_heads, step_size, b_state, decay_rate, doc_ids, prev_doc):
    log_decay = jnp.cumsum(step_size * decay_rate, axis=0)
    end_keep = (doc_ids == doc_ids[-1:]).astype(jnp.float32)
    weight = jnp.exp(log_decay[-1:] - log_decay) * end_keep[..., None] * step_size
    s_local = jnp.einsum("tsh,tshp,tsn->shpn", weight, x_heads, b_state, precision=HIGH)
    a_total = jnp.exp(log_decay[-1]) * (doc_ids[-1] == prev_doc).astype(jnp.float32)[:, None]
    return (s_local, a_total)


def group_output(x_heads, step_size, b_state, c_state, decay_rate, doc_ids, prev_doc, s_in):
    length_here = x_heads.shape[0]
    log_decay = jnp.cumsum(step_size * decay_rate, axis=0)
    causal = jnp.arange(length_here)[:, None] >= jnp.arange(length_here)[None, :]
    pair_mask = (causal[:, :, None] & (doc_ids[:, None, :] == doc_ids[None, :, :])).astype(
        jnp.float32
    )
    gap_decay = log_decay[:, None] - log_decay[None, :]
    decay_table = (
        jnp.exp(jnp.where(pair_mask[..., None] > 0, gap_decay, 0.0)) * pair_mask[..., None]
    )
    cross_dot = jnp.einsum("tsn,usn->tus", c_state, b_state, precision=HIGH)
    y_intra = jnp.einsum(
        "tush,ush,ushp->tshp",
        decay_table * cross_dot[..., None],
        step_size,
        x_heads,
        precision=HIGH,
    )
    enters = jnp.exp(log_decay) * (doc_ids == prev_doc[None, :]).astype(jnp.float32)[..., None]
    y_inter = jnp.einsum("tsn,shpn->tshp", c_state, s_in, precision=HIGH) * enters[..., None]
    return y_intra + y_inter


def ssm_local(x_heads, step_size, b_state, c_state, decay_rate, s_in, doc_ids, prev_doc):
    y_core = group_output(x_heads, step_size, b_state, c_state, decay_rate, doc_ids, prev_doc, s_in)
    s_local, a_total = group_parts(x_heads, step_size, b_state, decay_rate, doc_ids, prev_doc)
    return (y_core, a_total[..., None, None] * s_in + s_local)


def carry_combine(earlier, later_part):
    return (earlier[0] * later_part[0], later_part[0][..., None, None] * earlier[1] + later_part[1])


def head_total(partial_sum):
    return lax.psum(partial_sum, "head")


def flat_dot(left_side, right_side):
    lead_dims = left_side.shape[:-1]
    product = jnp.dot(
        left_side.reshape(-1, left_side.shape[-1]), right_side, preferred_element_type=jnp.float32
    )
    return product.reshape(lead_dims + (right_side.shape[-1],))


def flat_dot_t(left_side, right_side):
    lead_dims = left_side.shape[:-1]
    product = lax.dot_general(
        left_side.reshape(-1, left_side.shape[-1]),
        right_side,
        (((1,), (1,)), ((), ())),
        preferred_element_type=jnp.float32,
    )
    return product.reshape(lead_dims + (right_side.shape[0],))


def outer_sum(left_side, right_side):
    return lax.dot_general(
        left_side.reshape(-1, left_side.shape[-1]),
        right_side.reshape(-1, right_side.shape[-1]),
        (((0,), (0,)), ((), ())),
        preferred_element_type=jnp.float32,
    )


def silu_slope(values, sigmoid_of):
    return sigmoid_of * (1.0 + values * (1.0 - sigmoid_of))


def norm_back(grad_normed, values, scale_of, gain):
    scaled_grad = grad_normed * gain
    gain_grad = jnp.sum((grad_normed * values * scale_of).reshape(-1, values.shape[-1]), axis=0)
    cube = scale_of * scale_of * scale_of
    value_grad = scale_of * scaled_grad - values * cube * jnp.mean(
        scaled_grad * values, axis=-1, keepdims=True
    )
    return (value_grad, gain_grad)


def on_device(
    hidden_in,
    doc_ids,
    routes,
    norm1_gain,
    w_z,
    w_x,
    w_bc,
    w_dt,
    conv_x,
    conv_bc,
    convb_x,
    convb_bc,
    dt_bias,
    a_log,
    d_skip,
    gnorm_gain,
    w_out,
    norm2_gain,
    router,
    shared_gate,
    shared_up,
    shared_down,
    expert_gate,
    expert_up,
    expert_down,
    cotangent,
):
    block_len, seq_here, width = hidden_in.shape
    top_count = routes.shape[-1]
    heads_here = dt_bias.shape[0]
    inner_here = convb_x.shape[0]
    head_size = inner_here // heads_here
    state_size = convb_bc.shape[0] // 2
    seq_count = lax.axis_size("seq")
    local_experts = expert_gate.shape[0]
    experts_all = local_experts * seq_count
    tok_here = block_len * seq_here
    capacity = 2 * tok_here * top_count // experts_all
    edge_len = KER - 1
    x_float = hidden_in.astype(jnp.float32)
    scale_one = lax.rsqrt(jnp.mean(x_float * x_float, axis=-1, keepdims=True) + EPS)
    normed_one = (x_float * scale_one * norm1_gain).astype(jnp.bfloat16)
    gathered = (
        lax.all_gather(w_z, "seq", axis=0, tiled=True),
        lax.all_gather(w_x, "seq", axis=0, tiled=True),
        lax.all_gather(w_dt, "seq", axis=0, tiled=True),
        lax.all_gather(w_bc, "seq", axis=0, tiled=True),
        lax.all_gather(router, "seq", axis=0, tiled=True),
        lax.all_gather(shared_gate, "seq", axis=0, tiled=True),
        lax.all_gather(shared_up, "seq", axis=0, tiled=True),
        lax.all_gather(w_out, "seq", axis=1, tiled=True),
        lax.all_gather(shared_down, "seq", axis=1, tiled=True),
    )
    full_z, full_x, full_dt, full_bc, full_router, full_sgate, full_sup, full_out, full_sdown = (
        gathered
    )
    gate_z = flat_dot(normed_one, full_z)
    proj_x = flat_dot(normed_one, full_x)
    proj_bc = flat_dot(normed_one, full_bc)
    dt_pre = flat_dot(normed_one, full_dt) + dt_bias
    conv_in = jnp.concatenate([proj_x, proj_bc], axis=-1)
    tail_in, tail_doc = (
        passed_along(conv_in[block_len - edge_len :].astype(jnp.bfloat16), "seq", 1).astype(
            jnp.float32
        ),
        passed_along(
            doc_ids[block_len - edge_len :].astype(jnp.float32).astype(jnp.bfloat16), "seq", 1
        ).astype(jnp.float32),
    )
    conv_ext = jnp.concatenate([tail_in, conv_in], 0)
    docs_ext = jnp.concatenate([tail_doc.astype(jnp.int32), doc_ids], 0)
    conv_weight = jnp.concatenate([conv_x, conv_bc], -1)
    conv_shift = jnp.concatenate([convb_x, convb_bc], -1)
    conv_out = conv_apply(conv_ext, docs_ext, conv_weight, conv_shift)
    x_heads = conv_out[..., :inner_here].reshape(block_len, seq_here, heads_here, head_size)
    b_state = conv_out[..., inner_here : inner_here + state_size]
    c_state = conv_out[..., inner_here + state_size :]
    step_size = jax.nn.softplus(dt_pre)
    decay_rate = -jnp.exp(a_log)
    prev_doc = docs_ext[edge_len - 1]
    s_local, a_total = group_parts(x_heads, step_size, b_state, decay_rate, doc_ids, prev_doc)
    ones_start = jnp.ones_like(a_total)
    zeros_start = jnp.zeros_like(s_local)
    a_before, s_before = entering(
        (a_total, s_local), "seq", carry_combine, (ones_start, zeros_start), False
    )
    y_core = group_output(
        x_heads, step_size, b_state, c_state, decay_rate, doc_ids, prev_doc, s_before
    )
    y_heads = y_core + d_skip[:, None] * x_heads
    y_flat = y_heads.reshape(block_len, seq_here, inner_here)
    gate_sig = jax.nn.sigmoid(gate_z)
    gated = y_flat * gate_z * gate_sig
    square_sum = head_total(jnp.sum(gated * gated, axis=-1, keepdims=True))
    scale_gated = lax.rsqrt(square_sum / INNER + EPS)
    mixed_out = (gated * scale_gated * gnorm_gain).astype(jnp.bfloat16)
    residual = x_float + head_total(flat_dot(mixed_out, full_out))
    scale_two = lax.rsqrt(jnp.mean(residual * residual, axis=-1, keepdims=True) + EPS)
    normed_two = (residual * scale_two * norm2_gain).astype(jnp.bfloat16)
    logits = flat_dot(normed_two, full_router)
    gate_probs = jax.nn.softmax(jnp.take_along_axis(logits, routes, axis=-1), axis=-1)
    share_gate = flat_dot(normed_two, full_sgate)
    share_up = flat_dot(normed_two, full_sup)
    share_sig = jax.nn.sigmoid(share_gate)
    share_act = (share_gate * share_sig * share_up).astype(jnp.bfloat16)
    share_part = flat_dot(share_act, full_sdown)
    slot_total = tok_here * top_count
    route_flat = routes.reshape(slot_total)
    expert_ids = jnp.arange(experts_all, dtype=jnp.int32)
    route_hits = (route_flat[:, None] == expert_ids[None, :]).astype(jnp.int32)
    slot_rank = jnp.sum(jnp.cumsum(route_hits, axis=0) * route_hits, axis=1) - 1
    target = route_flat * capacity + slot_rank
    entry_table = (
        jnp.zeros((experts_all * capacity,), jnp.int32)
        .at[target]
        .set(jnp.arange(slot_total, dtype=jnp.int32) + 1)
    )
    entry_live = entry_table > 0
    entry_slot = jnp.maximum(entry_table - 1, 0)
    entry_token = entry_slot // top_count
    tokens_flat = normed_two.reshape(tok_here, width)
    send_rows = jnp.where(
        entry_live[:, None], tokens_flat[entry_token], jnp.zeros((), jnp.bfloat16)
    ).reshape(experts_all, capacity, width)
    received = lax.all_to_all(send_rows, "seq", split_axis=0, concat_axis=0, tiled=True)
    input_row_block = received.reshape(seq_count, local_experts, received.shape[1], width)
    hid_gate = jnp.einsum(
        "jecd,edf->jecf", input_row_block, expert_gate, preferred_element_type=jnp.float32
    )
    hid_up = jnp.einsum(
        "jecd,edf->jecf", input_row_block, expert_up, preferred_element_type=jnp.float32
    )
    hid_act = (hid_gate * jax.nn.sigmoid(hid_gate) * hid_up).astype(jnp.bfloat16)
    half_out = jnp.einsum(
        "jecf,efd->jecd", hid_act, expert_down, preferred_element_type=jnp.float32
    ).astype(jnp.bfloat16)
    returned_rows = lax.all_to_all(
        half_out.reshape(received.shape), "seq", split_axis=0, concat_axis=0, tiled=True
    )
    kept_shape = (seq_count * local_experts, received.shape[1], hid_gate.shape[-1])
    returned_rows, rows_kept, gate_kept, up_kept = (
        returned_rows,
        received,
        hid_gate.reshape(kept_shape),
        hid_up.reshape(kept_shape),
    )
    slot_rows = returned_rows.reshape(-1, width)[target].reshape(tok_here, top_count, width)
    probs_flat = gate_probs.reshape(tok_here, top_count)
    routed_part = share_part.reshape(tok_here, width)
    for slot_index in range(top_count):
        routed_part = routed_part + probs_flat[:, slot_index, None] * slot_rows[
            :, slot_index
        ].astype(jnp.float32)
    moe_out = head_total(routed_part.reshape(block_len, seq_here, width))
    block_out = residual + moe_out
    gathered = (
        lax.all_gather(w_z, "seq", axis=0, tiled=True),
        lax.all_gather(w_x, "seq", axis=0, tiled=True),
        lax.all_gather(w_dt, "seq", axis=0, tiled=True),
        lax.all_gather(w_bc, "seq", axis=0, tiled=True),
        lax.all_gather(router, "seq", axis=0, tiled=True),
        lax.all_gather(shared_gate, "seq", axis=0, tiled=True),
        lax.all_gather(shared_up, "seq", axis=0, tiled=True),
        lax.all_gather(w_out, "seq", axis=1, tiled=True),
        lax.all_gather(shared_down, "seq", axis=1, tiled=True),
    )
    full_z, full_x, full_dt, full_bc, full_router, full_sgate, full_sup, full_out, full_sdown = (
        gathered
    )
    grad_out = cotangent.astype(jnp.float32)
    grad_flat = grad_out.reshape(tok_here, width)
    entry_prob = jnp.where(entry_live, gate_probs.reshape(-1)[entry_slot], 0.0)
    send_grads = (
        (entry_prob[:, None] * grad_flat[entry_token])
        .astype(jnp.bfloat16)
        .reshape(experts_all, capacity, width)
    )
    recv_grads = lax.all_to_all(send_grads, "seq", split_axis=0, concat_axis=0, tiled=True)
    grads_in = recv_grads.reshape(seq_count, local_experts, capacity, width)
    input_row_block = rows_kept.reshape(seq_count, local_experts, capacity, width)
    hid_gate = gate_kept.reshape(seq_count, local_experts, capacity, -1)
    hid_up = up_kept.reshape(seq_count, local_experts, capacity, -1)
    hid_sig = jax.nn.sigmoid(hid_gate)
    hid_act = (hid_gate * hid_sig * hid_up).astype(jnp.bfloat16)
    d_act = jnp.einsum("jecd,efd->jecf", grads_in, expert_down, preferred_element_type=jnp.float32)
    hidden_up_gradient = (d_act * hid_gate * hid_sig).astype(jnp.bfloat16)
    d_hid_gate = (d_act * hid_up * silu_slope(hid_gate, hid_sig)).astype(jnp.bfloat16)
    grad_edown = jnp.einsum("jecf,jecd->efd", hid_act, grads_in, preferred_element_type=jnp.float32)
    grad_egate = jnp.einsum(
        "uqpy,uqpn->qyn", input_row_block, d_hid_gate, preferred_element_type=jnp.float32
    )
    expert_up_gradient = jnp.einsum(
        "uqpy,uqpn->qyn", input_row_block, hidden_up_gradient, preferred_element_type=jnp.float32
    )
    d_rows = jnp.einsum(
        "jecf,edf->jecd", d_hid_gate, expert_gate, preferred_element_type=jnp.float32
    )
    d_rows = (
        d_rows
        + jnp.einsum(
            "jecf,edf->jecd", hidden_up_gradient, expert_up, preferred_element_type=jnp.float32
        )
    ).astype(jnp.bfloat16)
    back_rows = lax.all_to_all(
        d_rows.reshape(recv_grads.shape), "seq", split_axis=0, concat_axis=0, tiled=True
    )
    d_share_act = flat_dot_t(cotangent, full_sdown)
    d_share_up = (d_share_act * share_gate * share_sig).astype(jnp.bfloat16)
    d_share_gate = (d_share_act * share_up * silu_slope(share_gate, share_sig)).astype(jnp.bfloat16)
    grad_sdown = outer_sum(share_act, cotangent)
    grad_sgate = outer_sum(normed_two, d_share_gate)
    grad_sup = outer_sum(normed_two, d_share_up)
    d_normed_two = (
        flat_dot_t(d_share_gate, full_sgate) + flat_dot_t(d_share_up, full_sup)
    ).reshape(tok_here, width)
    prob_grad = jnp.stack(
        [
            jnp.sum(grad_flat * slot_rows[:, slot_index].astype(jnp.float32), axis=-1)
            for slot_index in range(top_count)
        ],
        axis=-1,
    )
    back_slots = back_rows.reshape(-1, width)[target].reshape(tok_here, top_count, width)
    for slot_index in range(top_count):
        d_normed_two = d_normed_two + back_slots[:, slot_index].astype(jnp.float32)
    d_normed_two, prob_grad = head_total(
        (
            d_normed_two.reshape(block_len, seq_here, width),
            prob_grad.reshape(block_len, seq_here, top_count),
        )
    )
    d_chosen = gate_probs * (prob_grad - jnp.sum(gate_probs * prob_grad, axis=-1, keepdims=True))
    d_logits = jnp.sum(
        d_chosen[..., None] * (routes[..., None] == expert_ids).astype(jnp.float32), axis=-2
    ).astype(jnp.bfloat16)
    grad_router = outer_sum(normed_two, d_logits)
    d_normed_two = d_normed_two + flat_dot_t(d_logits, full_router)
    d_resid_norm, grad_norm2 = norm_back(d_normed_two, residual, scale_two, norm2_gain)
    d_resid = grad_out + d_resid_norm
    d_resid_low = d_resid.astype(jnp.bfloat16)
    d_mixed = flat_dot_t(d_resid_low, full_out)
    grad_out_w = outer_sum(mixed_out, d_resid_low)
    gain_scaled = d_mixed * gnorm_gain
    grad_gnorm = jnp.sum((d_mixed * gated * scale_gated).reshape(-1, inner_here), axis=0)
    cross_sum = head_total(jnp.sum(gain_scaled * gated, axis=-1, keepdims=True))
    d_gated = (
        scale_gated * gain_scaled
        - gated * scale_gated * scale_gated * scale_gated * cross_sum / INNER
    )
    d_y = d_gated * gate_z * gate_sig
    d_gate_z = (d_gated * y_flat * silu_slope(gate_z, gate_sig)).astype(jnp.bfloat16)
    d_y_heads = d_y.reshape(x_heads.shape)
    grad_skip = jnp.sum(d_y_heads * x_heads, axis=(0, 1, 3))
    log_decay = jnp.cumsum(step_size * decay_rate, axis=0)
    enters = jnp.exp(log_decay) * (doc_ids == prev_doc[None, :]).astype(jnp.float32)[..., None]
    g_local = jnp.einsum("tsh,tshp,tsn->shpn", enters, d_y_heads, c_state, precision=HIGH)
    a_after, state_grad = entering(
        (a_total, g_local), "seq", carry_combine, (ones_start, zeros_start), True
    )

    def local_scan(x_part, step_part, b_part, c_part, rate_part, state_part):
        return ssm_local(
            x_part, step_part, b_part, c_part, rate_part, state_part, doc_ids, prev_doc
        )

    _, scan_back = jax.vjp(local_scan, x_heads, step_size, b_state, c_state, decay_rate, s_before)
    d_xh, d_step, d_bstate, d_cstate, d_rate, _ = scan_back((d_y_heads, state_grad))
    d_xh = d_xh + d_skip[:, None] * d_y_heads
    d_bc = head_total(jnp.concatenate([d_bstate, d_cstate], axis=-1))
    d_dt_pre = d_step * jax.nn.sigmoid(dt_pre)
    grad_dtb = jnp.sum(d_dt_pre, axis=(0, 1))
    grad_alog = d_rate * decay_rate
    d_conv_out = jnp.concatenate([d_xh.reshape(block_len, seq_here, inner_here), d_bc], axis=-1)

    def local_conv(ext_part, weight_part, shift_part):
        return conv_apply(ext_part, docs_ext, weight_part, shift_part)

    _, conv_back = jax.vjp(local_conv, conv_ext, conv_weight, conv_shift)
    d_ext, grad_cweight, grad_cshift = conv_back(d_conv_out)
    from_next = passed_along(shortened(d_ext[:edge_len]), "seq", -1)
    d_conv_in = d_ext[edge_len:] + jnp.concatenate(
        [jnp.zeros((block_len - edge_len,) + from_next.shape[1:], jnp.float32), from_next], 0
    )
    d_proj_x = d_conv_in[..., :inner_here].astype(jnp.bfloat16)
    d_proj_bc = d_conv_in[..., inner_here:].astype(jnp.bfloat16)
    d_dt_low = d_dt_pre.astype(jnp.bfloat16)
    grad_wz = outer_sum(normed_one, d_gate_z)
    grad_wx = outer_sum(normed_one, d_proj_x)
    grad_wbc = outer_sum(normed_one, d_proj_bc)
    grad_wdt = outer_sum(normed_one, d_dt_low)
    head_first = jnp.where(lax.axis_index("head") == 0, 1.0, 0.0)
    d_normed_one = (
        flat_dot_t(d_gate_z, full_z) + flat_dot_t(d_proj_x, full_x) + flat_dot_t(d_dt_low, full_dt)
    )
    d_normed_one = head_total(d_normed_one + head_first * flat_dot_t(d_proj_bc, full_bc))
    d_x_norm, grad_norm1 = norm_back(d_normed_one, x_float, scale_one, norm1_gain)
    input_grad = d_resid + d_x_norm
    reduced = (
        lax.psum_scatter(grad_wz, "seq", scatter_dimension=0, tiled=True),
        lax.psum_scatter(grad_wx, "seq", scatter_dimension=0, tiled=True),
        lax.psum_scatter(grad_wdt, "seq", scatter_dimension=0, tiled=True),
        lax.psum_scatter(grad_wbc, "seq", scatter_dimension=0, tiled=True),
        lax.psum_scatter(grad_router, "seq", scatter_dimension=0, tiled=True),
        lax.psum_scatter(grad_sgate, "seq", scatter_dimension=0, tiled=True),
        lax.psum_scatter(grad_sup, "seq", scatter_dimension=0, tiled=True),
        lax.psum_scatter(grad_out_w, "seq", scatter_dimension=1, tiled=True),
        lax.psum_scatter(grad_sdown, "seq", scatter_dimension=1, tiled=True),
    )
    red_z, red_x, red_dt, red_bc, red_router, red_sgate, red_sup, red_out, red_sdown = reduced
    small_sums = lax.psum(
        (
            grad_norm1,
            grad_norm2,
            grad_cweight,
            grad_cshift,
            grad_dtb,
            grad_alog,
            grad_skip,
            grad_gnorm,
        ),
        "seq",
    )
    sum_norm1, sum_norm2, sum_cweight, sum_cshift, sum_dtb, sum_alog, sum_skip, sum_gnorm = (
        small_sums
    )
    return (
        block_out,
        input_grad,
        sum_norm1,
        red_z,
        red_x,
        red_bc,
        red_dt,
        sum_cweight[:, :inner_here],
        sum_cweight[:, inner_here:],
        sum_cshift[:inner_here],
        sum_cshift[inner_here:],
        sum_dtb,
        sum_alog,
        sum_skip,
        sum_gnorm,
        red_out,
        sum_norm2,
        red_router,
        red_sgate,
        red_sup,
        red_sdown,
        grad_egate,
        expert_up_gradient,
        grad_edown,
    )


def solution(mesh):
    placed = (
        P("seq", None, None),
        P("seq", None),
        P("seq", None, None),
        P(),
        P("seq", "head"),
        P("seq", "head"),
        P("seq", None),
        P("seq", "head"),
        P(None, "head"),
        P(),
        P("head"),
        P(),
        P("head"),
        P("head"),
        P("head"),
        P("head"),
        P("head", "seq"),
        P(),
        P("seq", None),
        P("seq", "head"),
        P("seq", "head"),
        P("head", "seq"),
        P("seq", None, "head"),
        P("seq", None, "head"),
        P("seq", "head", None),
        P("seq", None, None),
    )
    return jax.shard_map(
        on_device,
        mesh=mesh,
        in_specs=placed,
        out_specs=(
            P("seq", None, None),
            P("seq", None, None),
            P(),
            P("seq", "head"),
            P("seq", "head"),
            P("seq", None),
            P("seq", "head"),
            P(None, "head"),
            P(),
            P("head"),
            P(),
            P("head"),
            P("head"),
            P("head"),
            P("head"),
            P("head", "seq"),
            P(),
            P("seq", None),
            P("seq", "head"),
            P("seq", "head"),
            P("head", "seq"),
            P("seq", None, "head"),
            P("seq", None, "head"),
            P("seq", "head", None),
        ),
        check_vma=False,
    )
```

profile of v0, /device:TPU:15, one launch (start us, length us, event | category | flops | bytes accessed | tf_op | source)
XLA Modules:
  0.0 2756.8 jit_solution(16741514925692414379)
XLA Ops:
  12.0 22.6 all-gather.2
  38.7 42.5 %all_gather.56 = bf16[1536,256]{1,0:T(8,128)(2,1)S(1)} all-gather(bf16[96,256]{1,0:T(8,128)(2,1)S(1)} %copy-done.129), channel_id=1, replica_groups=mesh['seq'=16,'head'=2] {'seq'}, dimensions={0}, use_global_device_ids=true | all-gather | bytes 835584 | tf_op jit(solution)/shard_map/all_gather | solution.py:201
  82.2 19.6 all-gather.13.cloned.1.call-done
  125.1 22.9 all_gather.57
  149.2 120.9 %all-gather.25.cloned.1.call-done = bf16[32,24,64,128]{3,2,1,0:T(8,128)(2,1)} async-done(((bf16[2,24,64,128]{3,2,1,0:T(8,128)(2,1)}), bf16[32,24,64,128]{3,2,1,0:T(8,128)(2,1)}) %all-gather.25.cloned.1.call-update) | async-done | bytes 12582928 | tf_op jit(solution)/shard_map/all_gather | solution.py:23
  270.1 25.2 while.30
  301.6 51.0 %all-gather.15.cloned.1.call-done = bf16[1536,1536]{1,0:T(8,128)(2,1)} async-done(((bf16[96,1536]{1,0:T(8,128)(2,1)}), bf16[1536,1536]{1,0:T(8,128)(2,1)}) %all-gather.15.cloned.1.call-update) | async-done | bytes 4718608 | tf_op jit(solution)/shard_map/all_gather | solution.py:198
  360.8 73.6 %all-gather.17.cloned.1.call-done = bf16[1536,1536]{0,1:T(8,128)(2,1)} async-done(((bf16[1536,96]{0,1:T(8,128)(2,1)}), bf16[1536,1536]{0,1:T(8,128)(2,1)}) %all-gather.17.cloned.1.call-update) | async-done | bytes 4718608 | tf_op jit(solution)/shard_map/all_gather | solution.py:205
  443.5 16.7 all-reduce.18.cloned.1.call-done
  472.0 109.0 %all_to_all.20 = bf16[16,96,1536]{2,1,0:T(8,128)(2,1)S(1)} all-to-all(bf16[16,96,1536]{2,1,0:T(8,128)(2,1)S(1)} %broadcast_select_fusion), channel_id=1, replica_groups=mesh['seq'=16,'head'=2] {'seq'}, dimensions={0} | all-to-all | bytes 9437184 | tf_op jit(solution)/shard_map/all_to_all | solution.py:279
  595.6 119.3 %all-gather.3 = bf16[16,96,16]{1,2,0:T(8,128)(2,1)S(1)} all-gather(bf16[1,96,16]{1,2,0:T(8,128)(2,1)S(1)} %bitcast.403), channel_id=1, replica_groups=mesh['seq'=16,'head'=2] {'seq'}, dimensions={0}, use_global_device_ids=true | all-gather | bytes 52224 | tf_op jit(solution)/shard_map/all_gather | solution.py:202
  742.0 13.3 fusion.233
  769.0 11.3 psum.116
  800.0 119.7 %all-to-all-done.2 = bf16[16,96,1536]{2,1,0:T(8,128)(2,1)} async-done(((bf16[16,96,1536]{2,1,0:T(8,128)(2,1)}), bf16[16,96,1536]{2,1,0:T(8,128)(2,1)}, u32[]{:S(2)}, u32[]{:S(2)}) %all-to-all-start.2) | async-done | bytes 4718624 | tf_op jit(solution)/shard_map/all_to_all | solution.py:332
  939.1 107.4 %all-gather.19.cloned.1.call-done = bf16[1536,512]{1,0:T(8,128)(2,1)} async-done(((bf16[96,512]{1,0:T(8,128)(2,1)}), bf16[1536,512]{1,0:T(8,128)(2,1)}) %all-gather.19.cloned.1.call-update) | async-done | bytes 1572880 | tf_op jit(solution)/shard_map/all_gather | solution.py:203
  1048.3 57.4 %all-gather.23.cloned.1.call-done = bf16[512,1536]{0,1:T(8,128)(2,1)} async-done(((bf16[512,96]{0,1:T(8,128)(2,1)}), bf16[512,1536]{0,1:T(8,128)(2,1)}) %all-gather.23.cloned.1.call-update) | async-done | bytes 1572880 | tf_op jit(solution)/shard_map/all_gather | solution.py:206
  1109.8 9.0 gather_fusion.4
  1122.4 15.1 fusion.125
  1152.3 20.6 all-reduce.20.cloned.1.call-done
  1216.2 126.0 %all-gather.27.cloned.1.call-done = bf16[32,24,64,128]{3,2,1,0:T(8,128)(2,1)} async-done(((bf16[2,24,64,128]{3,2,1,0:T(8,128)(2,1)}), bf16[32,24,64,128]{3,2,1,0:T(8,128)(2,1)}) %all-gather.27.cloned.1.call-update) | async-done | bytes 12582928 | tf_op jit(solution)/shard_map/all_gather | solution.py:23
  1342.2 35.5 %while.31 = (s32[]{:T(128)}, f32[2,24,64,128]{3,2,1,0:T(8,128)S(1)}, s32[]{:T(128)}, bf16[16,2,24]{2,1,0:T(2,128)(2,1)}, bf16[16,2,24,64,128]{4,3,2,1,0:T(8,128)...) while((s32[]{:T(128)}, f32[2,24,64,128]{3,2,1,0:T(8,128)S(1)}, s32[]{:T(128)}, ...), condition=%wide.region_29.30_spmd.clone, body=%wide.region_28.29_spmd.clone.sunk | while | flops 1966136 | bytes 3932815 | solution.py:41
  1463.6 66.1 %reduce-scatter.30.cloned.1.call-done = f32[96,16]{1,0:T(8,128)} async-done(((f32[1536,16]{1,0:T(8,128)}), f32[96,16]{1,0:T(8,128)}) %reduce-scatter.30.cloned.1.call-update) | async-done | bytes 6160
  1544.3 111.2 %reduce-scatter.28.cloned.1.call-done = f32[96,24]{1,0:T(8,128)} async-done(((f32[1536,24]{1,0:T(8,128)}), f32[96,24]{1,0:T(8,128)}) %reduce-scatter.28.cloned.1.call-update) | async-done | bytes 9232
  1656.9 23.8 all-reduce.24.cloned.1.call-done
  1682.1 51.0 %all-reduce.11 = (f32[1536]{0:T(1024)}, f32[4,1792]{1,0:T(4,128)S(1)}, f32[1792]{0:T(1024)S(1)}, f32[24]{0:T(128)}, f32[24]{0:T(128)}, /*index=5*/f32[24]{0:T(128)}, f32[1536]{0:T(1024)}, f32[1536]{0:T(1024)}) all-reduce(f32[1536]{0:T(1024)S(1)} %get-tuple-element.504, ...), channel_id=1, replica_groups=mesh['seq'=16,'head'=2] {'seq'}, use_global_device_ids=true, to_apply=%region_42.43 | all-reduce | flops 13640 | bytes 109120 | tf_op jit(solution)/shard_map/psum | solution.py:464
  1739.6 77.0 %reduce-scatter.26.cloned.1.call-done = f32[512,96]{0,1:T(8,128)} async-done(((f32[512,1536]{0,1:T(8,128)}), f32[512,96]{0,1:T(8,128)}) %reduce-scatter.26.cloned.1.call-update) | async-done | bytes 196624 | tf_op jit(solution)/shard_map/reduce_scatter | solution.py:461
  1816.5 136.2 %reduce-scatter.24.cloned.1.call-done = f32[96,512]{1,0:T(8,128)} async-done(((f32[1536,512]{1,0:T(8,128)}), f32[96,512]{1,0:T(8,128)}) %reduce-scatter.24.cloned.1.call-update) | async-done | bytes 196624 | tf_op jit(solution)/shard_map/reduce_scatter | solution.py:459
  1952.8 136.1 %reduce-scatter.22.cloned.1.call-done = f32[96,512]{1,0:T(8,128)} async-done(((f32[1536,512]{1,0:T(8,128)}), f32[96,512]{1,0:T(8,128)}) %reduce-scatter.22.cloned.1.call-update) | async-done | bytes 196624 | tf_op jit(solution)/shard_map/reduce_scatter | solution.py:458
  2088.8 177.9 %reduce-scatter.20.cloned.1.call-done = f32[1536,96]{0,1:T(8,128)} async-done(((f32[1536,1536]{0,1:T(8,128)}), f32[1536,96]{0,1:T(8,128)}) %reduce-scatter.20.cloned.1.call-update) | async-done | bytes 589840 | tf_op jit(solution)/shard_map/reduce_scatter | solution.py:460
  2266.7 176.3 %reduce-scatter.14.cloned.1.call-done = f32[96,1536]{1,0:T(8,128)} async-done(((f32[1536,1536]{1,0:T(8,128)}), f32[96,1536]{1,0:T(8,128)}) %reduce-scatter.14.cloned.1.call-update) | async-done | bytes 589840 | tf_op jit(solution)/shard_map/reduce_scatter | solution.py:453
  2443.0 129.1 %reduce-scatter.18.cloned.1.call-done = f32[96,256]{1,0:T(8,128)} async-done(((f32[1536,256]{1,0:T(8,128)}), f32[96,256]{1,0:T(8,128)}) %reduce-scatter.18.cloned.1.call-update) | async-done | bytes 98320 | tf_op jit(solution)/shard_map/reduce_scatter | solution.py:456
  2572.1 177.6 %reduce-scatter.16.cloned.1.call-done = f32[96,1536]{1,0:T(8,128)} async-done(((f32[1536,1536]{1,0:T(8,128)}), f32[96,1536]{1,0:T(8,128)}) %reduce-scatter.16.cloned.1.call-update) | async-done | bytes 589840 | tf_op jit(solution)/shard_map/reduce_scatter | solution.py:454
  (700 shorter events, 398.6 us)
Async XLA Ops:
  7.2 578.7 %copy-start = (bf16[1,256,1536]{2,1,0:T(8,128)(2,1)S(1)}, bf16[1,256,1536]{2,1,0:T(8,128)(2,1)}, u32[]{:S(2)}) copy-start(bf16[1,256,1536]{2,1,0:T(8,128)(2,1)} %param.54) | copy-start | bytes 2359300
  7.3 94.5 %all-gather.13.cloned.1.call-start = ((), (), s32[]{:S(2)}) async-start(), calls=%async_computation.13 | async-start | bytes 5013504 | tf_op jit(solution)/shard_map/all_gather | solution.py:199
  8.0 262.1 %all-gather.25.cloned.1.call-start = ((), (), s32[]{:S(2)}) async-start(), calls=%async_computation.29 | async-start | bytes 13369344 | tf_op jit(solution)/shard_map/all_gather | solution.py:23
  8.8 72.7 %collective-permute-start.1 = (bf16[3,2]{0,1:T(2,128)(2,1)S(1)}, bf16[3,2]{0,1:T(2,128)(2,1)S(1)}, u32[]{:S(2)}, u32[]{:S(2)}) collective-permute-start(bf16[3,2]{0,1:T(2,128)(2,1)S(1)} %convert_convert_fusion.1), channel_id=1, source_target_pairs={{0,2},{2,4},{4,6},{6,8},{8,10},{10,12},{12,14},{14,16},{16,18},{18... | collective-permute-start | bytes 44 | tf_op jit(solution)/shard_map/ppermute | solution.py:17
  105.0 4.6 collective-permute-start
  119.4 233.2 %all-gather.15.cloned.1.call-start = ((), (), s32[]{:S(2)}) async-start(), calls=%async_computation.14 | async-start | bytes 5013504 | tf_op jit(solution)/shard_map/all_gather | solution.py:198
  120.1 314.3 %all-gather.17.cloned.1.call-start = ((), (), s32[]{:S(2)}) async-start(), calls=%async_computation.15 | async-start | bytes 5013504 | tf_op jit(solution)/shard_map/all_gather | solution.py:205
  120.7 339.5 %all-reduce.18.cloned.1.call-start = ((), (), s32[]{:S(2)}) async-start(), calls=%async_computation.16 | async-start | bytes 1572864 | tf_op jit(solution)/shard_map/psum | solution.py:109
  123.3 174.7 %copy-start.100 = (f32[64,2,24]{0,2,1:T(8,128)}, f32[64,2,24]{0,2,1:T(8,128)S(1)}, u32[]{:S(2)}) copy-start(f32[64,2,24]{0,2,1:T(8,128)S(1)} %copy.472) | copy-start | bytes 36868
  123.3 174.6 %copy-start.79 = (f32[64,2,24]{0,2,1:T(8,128)}, f32[64,2,24]{0,2,1:T(8,128)S(1)}, u32[]{:S(2)}) copy-start(f32[64,2,24]{0,2,1:T(8,128)S(1)} %copy.474) | copy-start | bytes 36868
  589.5 141.8 %all-to-all-start.1 = ((bf16[16,96,1536]{2,1,0:T(8,128)(2,1)}), bf16[16,96,1536]{2,1,0:T(8,128)(2,1)}, u32[]{:S(2)}, u32[]{:S(2)}) async-start(bf16[16,96,1536]{2,1,0:T(8,128)(2,1)} %convolution_convert_fusion), calls=%async_computation.1 | async-start | bytes 9437184 | tf_op jit(solution)/shard_map/all_to_all | solution.py:291
  794.0 125.8 %all-to-all-start.2 = ((bf16[16,96,1536]{2,1,0:T(8,128)(2,1)}), bf16[16,96,1536]{2,1,0:T(8,128)(2,1)}, u32[]{:S(2)}, u32[]{:S(2)}) async-start(bf16[16,96,1536]{2,1,0:T(8,128)(2,1)} %multiply_convert_fusion), calls=%async_computation.2 | async-start | bytes 9437184 | tf_op jit(solution)/shard_map/all_to_all | solution.py:332
  799.5 137.8 %all-gather.21.cloned.1.call-start = ((), (), s32[]{:S(2)}) async-start(), calls=%async_computation.18 | async-start | bytes 1671168 | tf_op jit(solution)/shard_map/all_gather | solution.py:204
  930.2 179.6 %all-to-all-start.3 = ((bf16[16,96,1536]{2,1,0:T(8,128)(2,1)}), bf16[16,96,1536]{2,1,0:T(8,128)(2,1)}, u32[]{:S(2)}, u32[]{:S(2)}) async-start(bf16[16,96,1536]{2,1,0:T(8,128)(2,1)} %add_convert_fusion), calls=%async_computation.3 | async-start | bytes 9437184 | tf_op jit(solution)/shard_map/all_to_all | solution.py:358
  935.7 110.8 %all-gather.19.cloned.1.call-start = ((), (), s32[]{:S(2)}) async-start(), calls=%async_computation.17 | async-start | bytes 1671168 | tf_op jit(solution)/shard_map/all_gather | solution.py:203
  936.5 169.3 %all-gather.23.cloned.1.call-start = ((), (), s32[]{:S(2)}) async-start(), calls=%async_computation.19 | async-start | bytes 1671168 | tf_op jit(solution)/shard_map/all_gather | solution.py:206
  937.2 235.6 %all-reduce.20.cloned.1.call-start = ((), (), s32[]{:S(2)}) async-start(), calls=%async_computation.20 | async-start | bytes 1572864 | tf_op jit(solution)/shard_map/psum | solution.py:109
  1151.4 190.8 %all-gather.27.cloned.1.call-start = ((), (), s32[]{:S(2)}) async-start(), calls=%async_computation.30 | async-start | bytes 13369344 | tf_op jit(solution)/shard_map/all_gather | solution.py:23
  1192.7 225.4 %all-reduce.22.cloned.1.call-start = ((), (), s32[]{:S(2)}) async-start(), calls=%async_computation.21 | async-start | bytes 262144 | tf_op jit(solution)/shard_map/psum | solution.py:109
  1383.8 145.9 %reduce-scatter.30.cloned.1.call-start = ((), (), s32[]{:S(2)}) async-start(), calls=%async_computation.32 | async-start | bytes 835584
  1385.3 270.2 %reduce-scatter.28.cloned.1.call-start = ((), (), s32[]{:S(2)}) async-start(), calls=%async_computation.31 | async-start | bytes 835584
  1421.4 6.6 collective-permute-start.2
  1426.1 254.7 %all-reduce.24.cloned.1.call-start = ((), (), s32[]{:S(2)}) async-start(), calls=%async_computation.33 | async-start | bytes 3145728 | tf_op jit(solution)/shard_map/psum | solution.py:109
  1435.6 381.0 %reduce-scatter.26.cloned.1.call-start = ((), (), s32[]{:S(2)}) async-start(), calls=%async_computation.28 | async-start | bytes 3342336 | tf_op jit(solution)/shard_map/reduce_scatter | solution.py:461
  1437.9 514.8 %reduce-scatter.24.cloned.1.call-start = ((), (), s32[]{:S(2)}) async-start(), calls=%async_computation.27 | async-start | bytes 3342336 | tf_op jit(solution)/shard_map/reduce_scatter | solution.py:459
  1441.1 647.7 %reduce-scatter.22.cloned.1.call-start = ((), (), s32[]{:S(2)}) async-start(), calls=%async_computation.26 | async-start | bytes 3342336 | tf_op jit(solution)/shard_map/reduce_scatter | solution.py:458
  1444.2 822.5 %reduce-scatter.20.cloned.1.call-start = ((), (), s32[]{:S(2)}) async-start(), calls=%async_computation.25 | async-start | bytes 10027008 | tf_op jit(solution)/shard_map/reduce_scatter | solution.py:460
  1450.5 992.4 %reduce-scatter.14.cloned.1.call-start = ((), (), s32[]{:S(2)}) async-start(), calls=%async_computation.22 | async-start | bytes 10027008 | tf_op jit(solution)/shard_map/reduce_scatter | solution.py:453
  1456.6 1115.5 %reduce-scatter.18.cloned.1.call-start = ((), (), s32[]{:S(2)}) async-start(), calls=%async_computation.24 | async-start | bytes 1671168 | tf_op jit(solution)/shard_map/reduce_scatter | solution.py:456
  1458.3 1291.4 %reduce-scatter.16.cloned.1.call-start = ((), (), s32[]{:S(2)}) async-start(), calls=%async_computation.23 | async-start | bytes 10027008 | tf_op jit(solution)/shard_map/reduce_scatter | solution.py:454
  1543.9 190.4 %copy-start.16 = (f32[64,2,1536]{2,0,1:T(8,128)S(1)}, f32[64,2,1536]{2,0,1:T(8,128)}, u32[]{:S(2)}) copy-start(f32[64,2,1536]{2,0,1:T(8,128)} %copy-done.14) | copy-start | bytes 2359300
  1737.7 1012.0 %copy-start.1 = (bf16[1,256,1536]{2,1,0:T(8,128)(2,1)S(1)}, bf16[1,256,1536]{2,1,0:T(8,128)(2,1)}, u32[]{:S(2)}) copy-start(bf16[1,256,1536]{2,1,0:T(8,128)(2,1)} %param.54) | copy-start | bytes 2359300
  (172 other events, 3677.1 us)
Sparse Core Ops, SparseCore 0:
  10.9 90.8 all-gather.12
  119.5 150.5 all-gather.24
  272.9 79.6 all-gather.14
  355.2 79.0 all-gather.16
  439.4 20.7 all-reduce.17
  803.1 110.3 all-gather.20
  939.7 106.7 all-gather.18
  1049.7 56.0 all-gather.22
  1151.5 21.2 all-reduce.19
  1192.8 149.2 all-gather.26
  1383.9 19.9 all-reduce.21
  1408.5 121.1 reduce-scatter.29
  1534.4 121.0 reduce-scatter.27
  1658.3 22.4 all-reduce.23
  1686.9 129.5 reduce-scatter.25
  1822.7 130.0 reduce-scatter.23
  1958.9 129.8 reduce-scatter.21
  2095.9 170.7 reduce-scatter.19
  2273.0 169.9 reduce-scatter.13
  2448.9 123.1 reduce-scatter.17
  2579.3 170.3 reduce-scatter.15
where the time goes:
time: 2770 us; the launch traced here: 2760 us
  waiting for transfers between devices  1930 us (70%)
  blocking collectives  385 us (14%)
  matrix products  143 us (5%)
  local copies, waits for them, and re-layouts  132 us (5%)
  other arithmetic  120 us (4%)
    all_gather x2, waiting for transfers between devices, entering(): lax.all_gather(part.astype(kind), axis)  247 us
    unnamed x23, waiting for transfers between devices  181 us
    reduce_scatter x1, waiting for transfers between devices, on_device(): lax.psum_scatter(grad_out_w, 'seq', scatter_dimension=1, tiled=True)  178 us
    reduce_scatter x1, waiting for transfers between devices, on_device(): lax.psum_scatter(grad_wx, 'seq', scatter_dimension=0, tiled=True)  178 us
    reduce_scatter x1, waiting for transfers between devices, on_device(): lax.psum_scatter(grad_wz, 'seq', scatter_dimension=0, tiled=True)  176 us
    reduce_scatter x1, waiting for transfers between devices, on_device(): lax.psum_scatter(grad_sup, 'seq', scatter_dimension=0, tiled=True)  136 us
    reduce_scatter x1, waiting for transfers between devices, on_device(): lax.psum_scatter(grad_sgate, 'seq', scatter_dimension=0, tiled=True)  136 us
    reduce_scatter x1, waiting for transfers between devices, on_device(): lax.psum_scatter(grad_wbc, 'seq', scatter_dimension=0, tiled=True)  129 us
  transfers between devices with their start and end apart: 27, of which 22 were waited for; matrix products, arithmetic and copies ran while one was open for 7% of the time, Pallas kernels for 0%

commit v1 on v0

--- a/solution.py
+++ b/solution.py
@@ -1,6 +1,10 @@
+import functools
+
 import jax
 import jax.numpy as jnp
 from jax import lax
+from jax.experimental import pallas as pl
+from jax.experimental.pallas import tpu as pltpu
 from jax.sharding import PartitionSpec as P
 
 KER = 4
@@ -505,7 +509,1029 @@
     )
 
 
+MESH = pl.DeviceIdType.MESH
+VMEM = pltpu.VMEM
+
+
+def peers():
+    here, side = lax.axis_index("seq"), lax.axis_index("head")
+    x, y, z = lax.rem(here, 2), lax.rem(here // 2, 2), here // 4
+    col = x + 2 * y
+    return here, side, z, col, (1 - x) + 2 * y, x + 2 * (1 - y), 3 - col
+
+
+def layers(z):
+    lo, hi = lax.rem(z, 2), z // 2
+    return [2 * (1 - hi if k & 2 else hi) + (1 - lo if k & 1 else lo) for k in range(4)]
+
+
+def greet(devices):
+    barrier = pltpu.get_barrier_semaphore()
+    for device in devices:
+        pl.semaphore_signal(barrier, inc=1, device_id=device, device_id_type=MESH)
+    pl.semaphore_wait(barrier, len(devices))
+
+
+class Mail:
+    def __init__(self, send, base=0):
+        self.send, self.sent, self.base = send, [], base
+
+    def put(self, src, dst, sem, to):
+        copy = pltpu.make_async_remote_copy(
+            src_ref=src,
+            dst_ref=dst,
+            send_sem=self.send.at[self.base + len(self.sent)],
+            recv_sem=sem,
+            device_id=to,
+            device_id_type=MESH,
+        )
+        copy.start()
+        self.sent.append(copy)
+
+    def arrived(self, dst, sem):
+        pltpu.make_async_remote_copy(
+            src_ref=dst,
+            dst_ref=dst,
+            send_sem=self.send.at[0],
+            recv_sem=sem,
+            device_id=(0, 0),
+            device_id_type=MESH,
+        ).wait_recv()
+
+    def finish(self):
+        for copy in self.sent:
+            copy.wait_send()
+
+
+def rows_at(ref, start, size, step):
+    return ref.at[pl.ds(pl.multiple_of(start, step), size)]
+
+
+def gather_steps(mail, own_ref, out_ref, recv, recv_half, rows, half):
+    here, side, z, col, cx, cy, cd = peers()
+    zs = layers(z)
+    base = 4 * z
+
+    def block(place):
+        return rows_at(out_ref, place * rows, rows, 16)
+
+    def part(place, which):
+        size = rows - half if which else half
+        return rows_at(out_ref, place * rows + which * half, size, 16)
+
+    mail.put(own_ref, block(here), recv.at[3], (base + cx, side))
+    mail.put(own_ref, block(here), recv.at[7], (base + cy, side))
+    for k in (1, 2, 3):
+        mail.put(own_ref, block(here), recv.at[k - 1], (4 * zs[k] + col, side))
+    yield
+    for k in range(4):
+        if k:
+            at = 4 * zs[k] + col
+            mail.arrived(block(at), recv.at[k - 1])
+            mail.put(block(at), block(at), recv.at[3 + k], (base + cx, side))
+            mail.put(block(at), block(at), recv.at[7 + k], (base + cy, side))
+            yield
+        at = 4 * zs[k] + cx
+        mail.arrived(block(at), recv.at[3 + k])
+        mail.put(part(at, 0), part(at, 0), recv_half.at[k], (base + cy, side))
+        at = 4 * zs[k] + cy
+        mail.arrived(block(at), recv.at[7 + k])
+        mail.put(part(at, 1), part(at, 1), recv_half.at[4 + k], (base + cx, side))
+        yield
+    for k in range(4):
+        at = 4 * zs[k] + cd
+        mail.arrived(part(at, 0), recv_half.at[k])
+        mail.arrived(part(at, 1), recv_half.at[4 + k])
+        yield
+
+
+def near(side):
+    here, side, z, col, cx, cy, cd = peers()
+    zs = layers(z)
+    return [(4 * z + cx, side), (4 * z + cy, side)] + [(4 * zs[k] + col, side) for k in (1, 2, 3)]
+
+
+def note_puts(mail, src_of, notes_out, recv_n):
+    here, side = peers()[:2]
+    for k in range(1, 16):
+        to = lax.rem(here + k, 16)
+        mail.put(src_of(to), notes_out.at[here], recv_n.at[here], (to, side))
+
+
+def note_waits(mail, notes_out, recv_n):
+    here = peers()[0]
+    for k in range(1, 16):
+        place = lax.rem(here + k, 16)
+        mail.arrived(notes_out.at[place], recv_n.at[place])
+
+
+def gather_kernel(rows, own_ref, note_ref, out_ref, notes_out, send, recv, recv_half, recv_n, local):
+    here, side = peers()[:2]
+    greet(same_side(side, here))
+    mine = pltpu.make_async_copy(own_ref, rows_at(out_ref, here * rows, rows, 16), local)
+    mine.start()
+    mail = Mail(send)
+    steps = gather_steps(mail, own_ref, out_ref, recv, recv_half, rows, rows // 2)
+    next(steps)
+    notes_out[here] = note_ref[...]
+    note_puts(mail, lambda to: note_ref, notes_out, recv_n)
+    for _ in steps:
+        pass
+    note_waits(mail, notes_out, recv_n)
+    mine.wait()
+    mail.finish()
+
+
+def gather_rows(block, note, number):
+    rows, width = block.shape
+    vmem = pl.BlockSpec(memory_space=VMEM)
+    return pl.pallas_call(
+        functools.partial(gather_kernel, rows),
+        out_shape=(
+            jax.ShapeDtypeStruct((16 * rows, width), block.dtype),
+            jax.ShapeDtypeStruct((16,) + note.shape, note.dtype),
+        ),
+        in_specs=[vmem, vmem],
+        out_specs=(vmem, vmem),
+        scratch_shapes=[
+            pltpu.SemaphoreType.DMA((34,)),
+            pltpu.SemaphoreType.DMA((11,)),
+            pltpu.SemaphoreType.DMA((8,)),
+            pltpu.SemaphoreType.DMA((16,)),
+            pltpu.SemaphoreType.DMA,
+        ],
+        compiler_params=pltpu.CompilerParams(
+            collective_id=number, has_side_effects=True, vmem_limit_bytes=48 << 20
+        ),
+        name=f"gather_{number}",
+    )(block, note)
+
+
+def reduce_steps(mail, part_ref, out_ref, got, sums, recv, rows):
+    here, side, z, col, cx, cy, cd = peers()
+    zs = layers(z)
+    base = 4 * z
+    half = rows // 2
+    got_a, got_b, got_x, got_y, got_z = got
+    sum_x, sum_y, sum_z = sums
+    to_x, to_y = (base + cx, side), (base + cy, side)
+    f32 = jnp.float32
+
+    def half_of(place, which):
+        return rows_at(part_ref, place * rows + which * half, half, half)
+
+    def far(k):
+        at = 4 * zs[k] + cd
+        mail.put(half_of(at, 0), got_a.at[k], recv.at[k], to_y)
+        mail.put(half_of(at, 1), got_b.at[k], recv.at[4 + k], to_x)
+
+    def plain(k):
+        mail.put(half_of(4 * zs[k] + cx, 1), got_x.at[k, pl.ds(half, half)], recv.at[12 + k], to_x)
+        mail.put(half_of(4 * zs[k] + cy, 0), got_y.at[k, pl.ds(0, half)], recv.at[16 + k], to_y)
+
+    def joined(k):
+        mail.arrived(got_a.at[k], recv.at[k])
+        total = half_of(4 * zs[k] + cx, 0)[...].astype(f32) + got_a[k].astype(f32)
+        sum_x[k] = total.astype(sum_x.dtype)
+        mail.put(sum_x.at[k], got_x.at[k, pl.ds(0, half)], recv.at[8 + k], to_x)
+        mail.arrived(got_b.at[k], recv.at[4 + k])
+        total = half_of(4 * zs[k] + cy, 1)[...].astype(f32) + got_b[k].astype(f32)
+        sum_y[k] = total.astype(sum_y.dtype)
+        mail.put(sum_y.at[k], got_y.at[k, pl.ds(half, half)], recv.at[20 + k], to_y)
+
+    def column(k):
+        mail.arrived(got_x.at[k, pl.ds(half, half)], recv.at[12 + k])
+        mail.arrived(got_y.at[k, pl.ds(0, half)], recv.at[16 + k])
+        mail.arrived(got_x.at[k, pl.ds(0, half)], recv.at[8 + k])
+        mail.arrived(got_y.at[k, pl.ds(half, half)], recv.at[20 + k])
+        own = part_ref[pl.ds(pl.multiple_of((4 * zs[k] + col) * rows, rows), rows)].astype(f32)
+        total = own + got_x[k].astype(f32) + got_y[k].astype(f32)
+        if k:
+            sum_z[k - 1] = total.astype(sum_z.dtype)
+            mail.put(sum_z.at[k - 1], got_z.at[k - 1], recv.at[23 + k], (4 * zs[k] + col, side))
+        else:
+            out_ref[...] = total
+
+    far(3)
+    plain(3)
+    yield
+    far(2)
+    plain(2)
+    yield
+    joined(3)
+    yield
+    far(1)
+    plain(1)
+    yield
+    joined(2)
+    yield
+    column(3)
+    yield
+    far(0)
+    plain(0)
+    yield
+    joined(1)
+    yield
+    column(2)
+    yield
+    joined(0)
+    yield
+    column(1)
+    yield
+    column(0)
+    yield
+    for k in (3, 2, 1):
+        mail.arrived(got_z.at[k - 1], recv.at[23 + k])
+        out_ref[...] += got_z[k - 1].astype(f32)
+
+
+def reduce_scratch(rows, width, kind):
+    half = rows // 2
+    shapes = [(4, half), (4, half), (4, rows), (4, rows), (3, rows), (4, half), (4, half), (3, rows)]
+    return [VMEM(shape + (width,), kind) for shape in shapes]
+
+
+def reduce_kernel(rows, part_ref, note_ref, out_ref, notes_out, *refs):
+    got, sums, (send, recv, recv_n) = refs[:5], refs[5:8], refs[8:]
+    here, side = peers()[:2]
+    greet(same_side(side, here))
+    mail = Mail(send)
+    steps = reduce_steps(mail, part_ref, out_ref, got, sums, recv, rows)
+    next(steps)
+    notes_out[here] = note_ref[here]
+    note_puts(mail, lambda to: note_ref.at[to], notes_out, recv_n)
+    for _ in steps:
+        pass
+    note_waits(mail, notes_out, recv_n)
+    mail.finish()
+
+
+def reduce_rows(parts, notes, number):
+    rows, width = parts.shape[0] // 16, parts.shape[1]
+    vmem = pl.BlockSpec(memory_space=VMEM)
+    return pl.pallas_call(
+        functools.partial(reduce_kernel, rows),
+        out_shape=(
+            jax.ShapeDtypeStruct((rows, width), jnp.float32),
+            jax.ShapeDtypeStruct(notes.shape, notes.dtype),
+        ),
+        in_specs=[vmem, vmem],
+        out_specs=(vmem, vmem),
+        scratch_shapes=reduce_scratch(rows, width, parts.dtype)
+        + [
+            pltpu.SemaphoreType.DMA((42,)),
+            pltpu.SemaphoreType.DMA((27,)),
+            pltpu.SemaphoreType.DMA((16,)),
+        ],
+        compiler_params=pltpu.CompilerParams(
+            collective_id=number, has_side_effects=True, vmem_limit_bytes=48 << 20
+        ),
+        name=f"reduce_{number}",
+    )(parts, notes)
+
+
+def same_side(side, here):
+    return [(lax.rem(here + k, 16), side) for k in range(1, 16)]
+
+
+def enter_kernel(
+    rows,
+    own_ref,
+    blocks_ref,
+    small_ref,
+    gate_ref,
+    up_ref,
+    down_ref,
+    all_ref,
+    extra_ref,
+    cols_ref,
+    small_other,
+    gate_other,
+    up_other,
+    down_other,
+    send,
+    recv,
+    recv_half,
+    recv_w,
+    recv_e,
+    recv_s,
+    local,
+):
+    here, side = peers()[:2]
+    places = 16
+    sibling = (here, 1 - side)
+    greet(same_side(side, here) + [sibling])
+    depth = blocks_ref.shape[1]
+    extra = rows - 64
+    half_here = here // 8
+    mail = Mail(send)
+    mine = pltpu.make_async_copy(own_ref, rows_at(all_ref, here * rows, rows, 16), local.at[0])
+    mine.start()
+
+    def strip(place):
+        return rows_at(cols_ref, place * depth, depth, 16)
+
+    steps = gather_steps(mail, own_ref, all_ref, recv, recv_half, rows, rows // 32 * 16)
+    next(steps)
+    mail.put(small_ref, small_other, recv_s.at[0], sibling)
+    away = []
+    for k in range(1, 8):
+        to = 8 * side + lax.rem(here + k, 8)
+        away.append(to)
+    first = 8 * side + lax.rem(here, 8)
+    is_mine = side == half_here
+    for k in range(1, 8):
+        to = 8 * side + lax.rem(here + k, 8)
+        mail.put(blocks_ref.at[to - 8 * side], strip(here), recv_w.at[here], (to, side))
+
+    @pl.when(is_mine)
+    def _():
+        pltpu.make_async_copy(blocks_ref.at[here - 8 * side], strip(here), local.at[1]).start()
+
+    @pl.when(jnp.logical_not(is_mine))
+    def _():
+        pltpu.make_async_remote_copy(
+            src_ref=blocks_ref.at[first - 8 * side],
+            dst_ref=strip(here),
+            send_sem=local.at[1],
+            recv_sem=recv_w.at[here],
+            device_id=(first, side),
+            device_id_type=MESH,
+        ).start()
+
+    mail.put(gate_ref, gate_other, recv_s.at[1], sibling)
+    mail.put(up_ref, up_other, recv_s.at[2], sibling)
+    mail.put(down_ref, down_other, recv_s.at[3], sibling)
+    for _ in steps:
+        pass
+    mine.wait()
+    for place in range(places):
+        src = all_ref.at[pl.ds(place * rows + 64, extra)]
+        mail.put(src, extra_ref.at[pl.ds(place * extra, extra)], recv_e.at[place], sibling)
+
+    def forward(place, sem):
+        return pltpu.make_async_remote_copy(
+            src_ref=strip(place),
+            dst_ref=strip(place),
+            send_sem=local.at[2 + sem],
+            recv_sem=recv_w.at[place],
+            device_id=sibling,
+            device_id_type=MESH,
+        )
+
+    @pl.when(is_mine)
+    def _():
+        pltpu.make_async_copy(blocks_ref.at[here - 8 * side], strip(here), local.at[1]).wait()
+        forward(here, 0).start()
+
+    @pl.when(jnp.logical_not(is_mine))
+    def _():
+        forward(here, 0).wait_recv()
+        pltpu.make_async_remote_copy(
+            src_ref=blocks_ref.at[first - 8 * side],
+            dst_ref=strip(here),
+            send_sem=local.at[1],
+            recv_sem=recv_w.at[here],
+            device_id=(first, side),
+            device_id_type=MESH,
+        ).wait_send()
+
+    for k in range(1, places):
+        place = lax.rem(here + k, places)
+        forward(place, k).wait_recv()
+
+        @pl.when(is_mine)
+        def _():
+            forward(place, k).start()
+
+    @pl.when(is_mine)
+    def _():
+        for k in range(places):
+            forward(lax.rem(here + k, places), k).wait_send()
+
+    mail.arrived(small_other, recv_s.at[0])
+    mail.arrived(gate_other, recv_s.at[1])
+    mail.arrived(up_other, recv_s.at[2])
+    mail.arrived(down_other, recv_s.at[3])
+    for place in range(places):
+        mail.arrived(extra_ref.at[pl.ds(place * extra, extra)], recv_e.at[place])
+    mail.finish()
+
+
+def enter(own, blocks, small, gate, up, down, number):
+    rows, width = own.shape
+    extra = rows - 64
+    depth, cols = blocks.shape[1:]
+    shape = jax.ShapeDtypeStruct
+    hbm = pl.BlockSpec(memory_space=pl.ANY)
+    vmem = pl.BlockSpec(memory_space=VMEM)
+    return pl.pallas_call(
+        functools.partial(enter_kernel, rows),
+        out_shape=(
+            shape((16 * rows, width), own.dtype),
+            shape((16 * extra, width), own.dtype),
+            shape((16 * depth, cols), blocks.dtype),
+            shape(small.shape, small.dtype),
+            shape(gate.shape, gate.dtype),
+            shape(up.shape, up.dtype),
+            shape(down.shape, down.dtype),
+        ),
+        in_specs=[vmem, vmem, vmem, hbm, hbm, hbm],
+        out_specs=(vmem, vmem, vmem, vmem, hbm, hbm, hbm),
+        scratch_shapes=[
+            pltpu.SemaphoreType.DMA((46,)),
+            pltpu.SemaphoreType.DMA((11,)),
+            pltpu.SemaphoreType.DMA((8,)),
+            pltpu.SemaphoreType.DMA((16,)),
+            pltpu.SemaphoreType.DMA((16,)),
+            pltpu.SemaphoreType.DMA((4,)),
+            pltpu.SemaphoreType.DMA((18,)),
+        ],
+        compiler_params=pltpu.CompilerParams(
+            collective_id=number, has_side_effects=True, vmem_limit_bytes=48 << 20
+        ),
+        name="enter",
+    )(own, blocks, small, gate, up, down)
+
+
+def leave_kernel(
+    main_ref,
+    bcr_ref,
+    small_ref,
+    main_out,
+    bcr_out,
+    small_out,
+    got_main,
+    got_bcr,
+    send_main,
+    send_bcr,
+    bcr_parts,
+    bcr_mine,
+    bcr_sib,
+    small_sum,
+    small_got,
+    send,
+    recv_sib,
+    recv_main,
+    recv_bcr,
+    recv_small,
+    cond,
+    local,
+):
+    here, side = peers()[:2]
+    sibling = (here, 1 - side)
+    half_here = here // 8
+    is_main = side == half_here
+    f32 = jnp.float32
+    greet(same_side(side, here) + [sibling])
+    mail = Mail(send)
+    depth = main_ref.shape[1]
+    mail.put(small_ref, small_got, recv_sib.at[1], sibling)
+
+    def give_main():
+        return pltpu.make_async_remote_copy(
+            src_ref=main_ref,
+            dst_ref=got_main,
+            send_sem=cond.at[0],
+            recv_sem=recv_sib.at[0],
+            device_id=sibling,
+            device_id_type=MESH,
+        )
+
+    def give_bcr():
+        return pltpu.make_async_remote_copy(
+            src_ref=bcr_ref,
+            dst_ref=got_bcr,
+            send_sem=cond.at[0],
+            recv_sem=recv_sib.at[0],
+            device_id=sibling,
+            device_id_type=MESH,
+        )
+
+    def send_on(total, out, sem, slot, k):
+        to = lax.rem(here + k, 16)
+        return pltpu.make_async_remote_copy(
+            src_ref=total.at[to],
+            dst_ref=out.at[slot],
+            send_sem=cond.at[k],
+            recv_sem=sem.at[slot],
+            device_id=(to, side),
+            device_id_type=MESH,
+        )
+
+    slot = lax.rem(here, 8)
+
+    @pl.when(is_main)
+    def _():
+        give_bcr().start()
+
+    @pl.when(jnp.logical_not(is_main))
+    def _():
+        give_main().start()
+
+    mail.arrived(small_got, recv_sib.at[1])
+    small_sum[...] = small_ref[...] + small_got[...]
+    small_out[here] = small_sum[...]
+    for k in range(1, 16):
+        to = lax.rem(here + k, 16)
+        mail.put(small_sum, small_out.at[here], recv_small.at[here], (to, side))
+
+    @pl.when(is_main)
+    def _():
+        give_main().wait_recv()
+        for k in range(1, 16):
+            to = lax.rem(here + k, 16)
+            total = main_ref[to].astype(f32) + got_main[to].astype(f32)
+            send_main[to] = total.astype(send_main.dtype)
+            send_on(send_main, main_out, recv_main, slot, k).start()
+        total = main_ref[here].astype(f32) + got_main[here].astype(f32)
+        main_out[slot] = total.astype(main_out.dtype)
+
+    @pl.when(jnp.logical_not(is_main))
+    def _():
+        give_bcr().wait_recv()
+        for k in range(1, 16):
+            to = lax.rem(here + k, 16)
+            total = bcr_ref[to].astype(f32) + got_bcr[to].astype(f32)
+            send_bcr[to] = total.astype(send_bcr.dtype)
+            send_on(send_bcr, bcr_parts, recv_bcr, slot, k).start()
+        total = bcr_ref[here].astype(f32) + got_bcr[here].astype(f32)
+        bcr_parts[slot] = total.astype(bcr_parts.dtype)
+
+    for j in range(8):
+        from_main = 8 * side + j
+        from_bcr = 8 * (1 - side) + j
+
+        @pl.when(from_bcr != here)
+        def _():
+            mail.arrived(bcr_parts.at[j], recv_bcr.at[j])
+
+    total = bcr_parts[0].astype(f32)
+    for j in range(1, 8):
+        total = total + bcr_parts[j].astype(f32)
+    bcr_mine[...] = total
+    mail.put(bcr_mine, bcr_sib, recv_sib.at[2], sibling)
+    for j in range(8):
+        from_main = 8 * side + j
+
+        @pl.when(from_main != here)
+        def _():
+            mail.arrived(main_out.at[j], recv_main.at[j])
+
+    for k in range(1, 16):
+        place = lax.rem(here + k, 16)
+        mail.arrived(small_out.at[place], recv_small.at[place])
+    mail.arrived(bcr_sib, recv_sib.at[2])
+    bcr_out[...] = bcr_mine[...] + bcr_sib[...]
+
+    @pl.when(is_main)
+    def _():
+        give_bcr().wait_send()
+        for k in range(1, 16):
+            send_on(send_main, main_out, recv_main, slot, k).wait_send()
+
+    @pl.when(jnp.logical_not(is_main))
+    def _():
+        give_main().wait_send()
+        for k in range(1, 16):
+            send_on(send_bcr, bcr_parts, recv_bcr, slot, k).wait_send()
+
+    mail.finish()
+
+
+def leave(main, bcr, small, number):
+    shape = jax.ShapeDtypeStruct
+    vmem = pl.BlockSpec(memory_space=VMEM)
+    low = jnp.bfloat16
+    return pl.pallas_call(
+        leave_kernel,
+        out_shape=(
+            shape((8,) + main.shape[1:], low),
+            shape(bcr.shape[1:], jnp.float32),
+            shape((16,) + small.shape, jnp.float32),
+        ),
+        in_specs=[vmem] * 3,
+        out_specs=(vmem, vmem, vmem),
+        scratch_shapes=[
+            VMEM(main.shape, low),
+            VMEM(bcr.shape, low),
+            VMEM(main.shape, low),
+            VMEM(bcr.shape, low),
+            VMEM((8,) + bcr.shape[1:], low),
+            VMEM(bcr.shape[1:], jnp.float32),
+            VMEM(bcr.shape[1:], jnp.float32),
+            VMEM(small.shape, jnp.float32),
+            VMEM(small.shape, jnp.float32),
+            pltpu.SemaphoreType.DMA((17,)),
+            pltpu.SemaphoreType.DMA((3,)),
+            pltpu.SemaphoreType.DMA((8,)),
+            pltpu.SemaphoreType.DMA((8,)),
+            pltpu.SemaphoreType.DMA((16,)),
+            pltpu.SemaphoreType.DMA((16,)),
+            pltpu.SemaphoreType.DMA,
+        ],
+        compiler_params=pltpu.CompilerParams(
+            collective_id=number, has_side_effects=True, vmem_limit_bytes=56 << 20
+        ),
+        name="leave",
+    )(main, bcr, small)
+
+
+def swap_kernel(count, *refs):
+    own, other, (send, recv) = refs[:count], refs[count : 2 * count], refs[2 * count :]
+    here, side = peers()[:2]
+    greet([(here, 1 - side)])
+    mail = Mail(send)
+    for i in range(count):
+        mail.put(own[i], other[i], recv.at[i], (here, 1 - side))
+    for i in range(count):
+        mail.arrived(other[i], recv.at[i])
+    mail.finish()
+
+
+def swap(arrays, number):
+    count = len(arrays)
+    hbm = pl.BlockSpec(memory_space=pl.ANY)
+    return pl.pallas_call(
+        functools.partial(swap_kernel, count),
+        out_shape=tuple(jax.ShapeDtypeStruct(a.shape, a.dtype) for a in arrays),
+        in_specs=[hbm] * count,
+        out_specs=(hbm,) * count,
+        scratch_shapes=[
+            pltpu.SemaphoreType.DMA((count,)),
+            pltpu.SemaphoreType.DMA((count,)),
+        ],
+        compiler_params=pltpu.CompilerParams(collective_id=number, has_side_effects=True),
+        name=f"swap_{number}",
+    )(*arrays)
+
+
+def chunked(array, chunk):
+    return array.reshape((array.shape[0] // chunk, chunk) + array.shape[1:])
+
+
+def scan_core(x_heads, step_size, b_state, c_state, decay_rate, doc_ids, chunk):
+    length = doc_ids.shape[0]
+    prev_all = jnp.concatenate([doc_ids[:1], doc_ids[:-1]], 0)
+    docs, prev = chunked(doc_ids, chunk), chunked(prev_all, chunk)[:, :1]
+    x_c, step_c = chunked(x_heads, chunk), chunked(step_size, chunk)
+    b_c, c_c = chunked(b_state, chunk), chunked(c_state, chunk)
+    logs = jnp.cumsum(step_c * decay_rate, axis=1)
+    causal = jnp.arange(chunk)[:, None] >= jnp.arange(chunk)[None, :]
+    pair = causal[None] & (docs[:, :, None] == docs[:, None, :])
+    logs_h = logs.transpose(0, 2, 1)
+    gap = logs_h[:, :, :, None] - logs_h[:, :, None, :]
+    table = jnp.exp(jnp.where(pair[:, None], gap, 0.0)) * pair[:, None].astype(jnp.float32)
+    cross = jnp.einsum("gtn,gun->gtu", c_c, b_c, precision=HIGH)
+    weights = table * cross[:, None] * step_c.transpose(0, 2, 1)[:, :, None, :]
+    intra = jnp.einsum("ghtu,guhp->gthp", weights, x_c, precision=HIGH)
+    enters = jnp.exp(logs) * (docs == prev).astype(jnp.float32)[..., None]
+    end_keep = (docs == docs[:, -1:]).astype(jnp.float32)
+    tail = jnp.exp(logs[:, -1:] - logs) * end_keep[..., None] * step_c
+    local = jnp.einsum("gth,gthp,gtn->ghpn", tail, x_c, b_c, precision=HIGH)
+    keep = enters[:, -1]
+    state = jnp.zeros_like(local[0])
+    before = []
+    for group in range(length // chunk):
+        before.append(state)
+        state = keep[group][:, None, None] * state + local[group]
+    before = jnp.stack(before)
+    inter = jnp.einsum("gtn,ghpn->gthp", c_c, before, precision=HIGH) * enters[..., None]
+    return (intra + inter).reshape(x_heads.shape)
+
+
+def by_heads(
+    hidden_in,
+    doc_ids,
+    routes,
+    norm1_gain,
+    w_z,
+    w_x,
+    w_bc,
+    w_dt,
+    conv_x,
+    conv_bc,
+    convb_x,
+    convb_bc,
+    dt_bias,
+    a_log,
+    d_skip,
+    gnorm_gain,
+    w_out,
+    norm2_gain,
+    router,
+    shared_gate,
+    shared_up,
+    shared_down,
+    expert_gate,
+    expert_up,
+    expert_down,
+    cotangent,
+):
+    places = lax.axis_size("seq")
+    here, side = lax.axis_index("seq"), lax.axis_index("head")
+    block_len, _, width = hidden_in.shape
+    length = block_len * places
+    heads_all = 2 * dt_bias.shape[0]
+    heads = heads_all // places
+    inner = 2 * convb_x.shape[0]
+    chans = inner // places
+    head_size = chans // heads
+    state = convb_bc.shape[0] // 2
+    shared_all = 2 * shared_gate.shape[1]
+    shared = shared_all // places
+    experts = router.shape[1]
+    top_count = routes.shape[-1]
+    hidden = 2 * expert_gate.shape[2]
+
+    half_here, slot = here // 8, lax.rem(here, 8)
+    low, f32 = jnp.bfloat16, jnp.float32
+
+    def mine_of(own, other):
+        return jnp.where(side == half_here, own, other)
+
+    def ordered(own, other, axis):
+        pair = jnp.where(side == 0, jnp.stack([own, other], axis), jnp.stack([other, own], axis))
+        return pair
+
+    def padded(array, rows):
+        flat = array.reshape(-1)
+        return jnp.pad(flat, (0, rows * width - flat.shape[0])).reshape(rows, width)
+
+    x_own = lax.dynamic_index_in_dim(hidden_in, side, 1, False).astype(f32)
+    g_own = lax.dynamic_index_in_dim(cotangent, side, 1, False)
+    scale_one = lax.rsqrt(jnp.mean(x_own * x_own, axis=-1, keepdims=True) + EPS)
+    n1_own = (x_own * scale_one * norm1_gain).astype(low)
+    ids = jnp.concatenate([doc_ids[:, :, None], routes], 2)
+    ids = lax.dynamic_index_in_dim(ids, side, 1, False)
+    bc_half = lax.dynamic_slice_in_dim(w_bc, side * state, state, 1)
+    own_rows = jnp.concatenate(
+        [
+            n1_own,
+            bc_half.reshape(8, width),
+            router.reshape(1, width),
+            padded(w_dt, 2),
+            padded(ids.astype(low), 1),
+            jnp.zeros((4, width), low),
+        ],
+        0,
+    )
+    blocks = jnp.concatenate(
+        [
+            part.reshape(part.shape[0], 8, part.shape[1] // 8)
+            for part in (w_z, w_x, shared_gate, shared_up, w_out.T, shared_down.T)
+        ],
+        2,
+    ).transpose(1, 0, 2)
+    small = jnp.concatenate(
+        [
+            conv_x,
+            convb_x[None],
+            gnorm_gain[None],
+            jnp.pad(jnp.concatenate([dt_bias, a_log, d_skip]), (0, width - 72))[None],
+            jnp.zeros((1, width), f32),
+        ],
+        0,
+    )
+    eg, eu, ed = expert_gate[0], expert_up[0], expert_down[0]
+    all_rows, extra_sib, cols, small_sib, eg_o, eu_o, ed_o = enter(
+        own_rows, blocks, small, eg, eu, ed, 1
+    )
+    all_rows = all_rows.reshape(places, 80, width)
+    extra_sib = extra_sib.reshape(places, 16, width)
+    n1 = all_rows[:, :block_len].reshape(length, width)
+    extra_own = all_rows[:, block_len:]
+    wbc = ordered(
+        extra_own[:, :8].reshape(width, state), extra_sib[:, :8].reshape(width, state), 1
+    ).reshape(width, 2 * state)
+    wrouter = extra_own[:, 8].reshape(width, experts)
+    wdt = mine_of(extra_own[:, 9:11], extra_sib[:, 9:11]).reshape(places, 2 * width)
+    wdt = wdt[:, : w_dt.shape[0] * w_dt.shape[1]].reshape(width, w_dt.shape[1])
+    wdt = lax.dynamic_slice_in_dim(wdt, slot * heads, heads, 1)
+    ids = extra_own[:, 11, : block_len * 7].reshape(length, 7).astype(jnp.int32)
+    docs, picks = ids[:, 0], ids[:, 1:]
+    small = mine_of(small, small_sib)
+    wide_small = lax.dynamic_slice_in_dim(small, slot * chans, chans, 1)
+    taps = jnp.concatenate([wide_small[:KER], conv_bc], 1)
+    shift = jnp.concatenate([wide_small[KER], convb_bc], 0)
+    gn_gain = wide_small[KER + 1]
+    head_params = small[KER + 2, :72].reshape(3, 24)
+    head_params = lax.dynamic_slice_in_dim(head_params, slot * heads, heads, 1)
+    bias_dt, rate_log, skip = head_params[0], head_params[1], head_params[2]
+    wz, wx, sg, su = cols[:, :192], cols[:, 192:384], cols[:, 384:448], cols[:, 448:512]
+    wout_t, sd_t = cols[:, 512:704], cols[:, 704:768]
+
+    def note(values):
+        return jnp.pad(values.reshape(1, block_len), ((0, 7), (0, 128 - block_len)))
+
+    def notes(values):
+        return jnp.pad(
+            values.reshape(places, 1, block_len), ((0, 0), (0, 7), (0, 128 - block_len))
+        )
+
+    def noted(array):
+        return array[:, 0, :block_len]
+
+    win = jnp.concatenate([wz, wx, wbc, wdt], 1)
+    proj = flat_dot(n1, win)
+    gate_z = proj[:, :chans]
+    conv_in = proj[:, chans : 2 * chans + 2 * state]
+    dt_pre = proj[:, 2 * chans + 2 * state :] + bias_dt
+    conv_ext = jnp.concatenate([jnp.zeros((KER - 1, conv_in.shape[1]), jnp.float32), conv_in], 0)
+    docs_ext = jnp.concatenate([jnp.full((KER - 1,), -1, jnp.int32), docs], 0)
+
+    def local_conv(ext_part, weight_part, shift_part):
+        return conv_apply(ext_part, docs_ext, weight_part, shift_part)
+
+    conv_out, conv_back = jax.vjp(local_conv, conv_ext, taps, shift)
+    x_heads = conv_out[:, :chans].reshape(length, heads, head_size)
+    b_state = conv_out[:, chans : chans + state]
+    c_state = conv_out[:, chans + state :]
+    step_size = jax.nn.softplus(dt_pre)
+    decay_rate = -jnp.exp(rate_log)
+
+    def local_scan(x_part, step_part, b_part, c_part, rate_part):
+        return scan_core(x_part, step_part, b_part, c_part, rate_part, docs, 128)
+
+    core, scan_back = jax.vjp(local_scan, x_heads, step_size, b_state, c_state, decay_rate)
+    y_flat = (core + skip[:, None] * x_heads).reshape(length, chans)
+    gate_sig = jax.nn.sigmoid(gate_z)
+    gated = y_flat * gate_z * gate_sig
+    gained = (gated * gn_gain).astype(jnp.bfloat16)
+    out_part = flat_dot_t(gained, wout_t)
+    out_sum, squares = reduce_rows(out_part.astype(low), notes(jnp.sum(gated * gated, axis=-1)), 2)
+    scale_own = lax.rsqrt(jnp.sum(noted(squares), axis=0) / inner + EPS)[:, None]
+    out_own = scale_own * out_sum
+    residual = x_own + out_own
+
+    scale_two = lax.rsqrt(jnp.mean(residual * residual, axis=-1, keepdims=True) + EPS)
+    n2_own = (residual * scale_two * norm2_gain).astype(jnp.bfloat16)
+    n2, scale_gated = gather_rows(n2_own, note(scale_own), 3)
+    scale_gated = noted(scale_gated).reshape(length, 1)
+    g_all, _ = gather_rows(g_own, note(scale_own), 4)
+    wup = jnp.concatenate([eg, eg_o, sg, eu, eu_o, su], 1)
+    wdown = jnp.concatenate([ed, ed_o, sd_t.T], 0)
+    wide = hidden + shared
+    logits = flat_dot(n2, wrouter)
+    named = jnp.sum((picks[:, :, None] == jnp.arange(experts)).astype(jnp.float32), axis=1)
+    top = jnp.max(jnp.where(named > 0, logits, -jnp.inf), axis=-1, keepdims=True)
+    raised = jnp.exp(jnp.where(named > 0, logits - top, 0.0)) * named
+    probs = raised / jnp.sum(raised, axis=-1, keepdims=True)
+    prob = lax.dynamic_slice_in_dim(probs, here, 1, 1)
+    col_prob = jnp.concatenate(
+        [jnp.broadcast_to(prob, (length, hidden)), jnp.ones((length, shared), jnp.float32)], 1
+    )
+    hid = flat_dot(n2, wup)
+    h_gate, h_up = hid[:, :wide], hid[:, wide:]
+    h_sig = jax.nn.sigmoid(h_gate)
+    act = h_gate * h_sig * h_up
+    act_low = (act * col_prob).astype(jnp.bfloat16)
+    moe_part = flat_dot(act_low, wdown)
+    block_sum, _ = reduce_rows(moe_part.astype(low), notes(jnp.zeros((length,), f32)), 5)
+    block_own = residual + block_sum
+
+    d_act = flat_dot_t(g_all, wdown)
+    prob_grad = jnp.sum((act * d_act)[:, :hidden], axis=-1)
+    d_act = d_act * col_prob
+    d_up = d_act * h_gate * h_sig
+    d_gate = d_act * h_up * silu_slope(h_gate, h_sig)
+    d_hid = jnp.concatenate([d_gate, d_up], 1).astype(jnp.bfloat16)
+    grad_down = outer_sum(act_low, g_all)
+    grad_up = outer_sum(n2, d_hid)
+    dn2_part = flat_dot_t(d_hid, wup)
+    dn2, prob_grads = reduce_rows(dn2_part.astype(low), notes(prob_grad), 6)
+    prob_grads = noted(prob_grads).T
+    probs_own = lax.dynamic_slice_in_dim(probs, here * block_len, block_len, 0)
+    d_logits = (
+        probs_own * (prob_grads - jnp.sum(probs_own * prob_grads, axis=-1, keepdims=True))
+    ).astype(jnp.bfloat16)
+    grad_router = outer_sum(n2_own, d_logits)
+    dn2 = dn2 + flat_dot_t(d_logits, wrouter)
+    d_norm, grad_norm2 = norm_back(dn2, residual, scale_two, norm2_gain)
+    d_res = g_own.astype(jnp.float32) + d_norm
+    d_res_low = d_res.astype(jnp.bfloat16)
+
+    cross_own = jnp.sum(d_res_low.astype(jnp.float32) * out_own, axis=-1, keepdims=True) / scale_own
+    d_res_all, cross = gather_rows(d_res_low, note(cross_own), 7)
+    cross = noted(cross).reshape(length, 1)
+    d_mixed = flat_dot(d_res_all, wout_t)
+    mixed_out = (gated * scale_gated * gn_gain).astype(jnp.bfloat16)
+    grad_out_t = outer_sum(d_res_all, mixed_out)
+    grad_gnorm = jnp.sum(d_mixed * gated * scale_gated, axis=0)
+    d_gated = scale_gated * gn_gain * d_mixed - gated * (
+        scale_gated * scale_gated * scale_gated * cross / inner
+    )
+    d_y = d_gated * gate_z * gate_sig
+    d_z = (d_gated * y_flat * silu_slope(gate_z, gate_sig)).astype(jnp.bfloat16)
+    d_y_heads = d_y.reshape(x_heads.shape)
+    grad_skip = jnp.sum(d_y_heads * x_heads, axis=(0, 2))
+    d_xh, d_step, d_b, d_c, d_rate = scan_back(d_y_heads)
+    d_xh = d_xh + skip[:, None] * d_y_heads
+    d_dt = d_step * jax.nn.sigmoid(dt_pre)
+    grad_dtb = jnp.sum(d_dt, axis=0)
+    grad_alog = d_rate * decay_rate
+    d_conv = jnp.concatenate([d_xh.reshape(length, chans), d_b, d_c], 1)
+    d_ext, grad_taps, grad_shift = conv_back(d_conv)
+    d_in = jnp.concatenate(
+        [d_z, d_ext[KER - 1 :].astype(jnp.bfloat16), d_dt.astype(jnp.bfloat16)], 1
+    )
+    grad_in = outer_sum(n1, d_in)
+    dn1, _ = reduce_rows(flat_dot_t(d_in, win).astype(low), notes(jnp.zeros((length,), f32)), 8)
+    d_x, grad_norm1 = norm_back(dn1, x_own, scale_one, norm1_gain)
+    input_own = d_res + d_x
+
+    grads = jnp.concatenate(
+        [
+            grad_in[:, : 2 * chans],
+            grad_up[:, hidden:wide],
+            grad_up[:, wide + hidden :],
+            grad_out_t,
+            grad_down[hidden:].T,
+        ],
+        1,
+    ).astype(low)
+    main = grads.reshape(places, 96, 768)
+    bcr = jnp.concatenate(
+        [
+            grad_in[:, 2 * chans : 2 * chans + 2 * state].reshape(places, 96, 256),
+            grad_router.reshape(places, 6, 256),
+            jnp.zeros((places, 10, 256), f32),
+        ],
+        1,
+    ).astype(low)
+    grad_wdt = grad_in[:, 2 * chans + 2 * state :]
+    singles = jnp.concatenate(
+        [
+            grad_norm1,
+            grad_norm2,
+            grad_taps[:, chans:].reshape(-1),
+            grad_shift[chans:],
+            grad_taps[:, :chans].reshape(-1),
+            grad_shift[:chans],
+            grad_gnorm,
+            grad_dtb,
+            grad_alog,
+            grad_skip,
+            grad_wdt.reshape(-1),
+        ]
+    )
+    singles = jnp.pad(singles, (0, 88 * 128 - singles.shape[0])).reshape(88, 128)
+    main, bcr, singles = leave(main, bcr, singles, 9)
+    singles = singles.reshape(places, -1)
+    sums = jnp.sum(singles[:, :4352], axis=0)
+    sums = jnp.split(sums, [1536, 3072, 4096])
+    lists = lax.dynamic_slice_in_dim(singles, 8 * side, 8, 0)[:, 4352:]
+    lists = jnp.split(lists, [768, 960, 1152, 1155, 1158, 1161, 1161 + 4608], axis=1)
+
+    def joined(part):
+        return part.transpose(1, 0, 2).reshape(part.shape[1], -1)
+
+    main = main.astype(f32)
+    bc_sum = bcr[:96]
+    router_sum = bcr[96:102].reshape(96, experts)
+    wdt_sum = joined(lists[6].reshape(8, width, heads))
+    wdt_sum = lax.dynamic_slice_in_dim(wdt_sum, here * 96, 96, 0)
+    other = swap(
+        (
+            block_own,
+            input_own,
+            grad_up[:, 256:512].astype(low),
+            grad_up[:, wide + 256 : wide + 512].astype(low),
+            grad_down[256:512].astype(low),
+        ),
+        10,
+    )
+    return (
+        ordered(block_own, other[0], 1),
+        ordered(input_own, other[1], 1),
+        sums[0],
+        joined(main[:, :, :192]),
+        joined(main[:, :, 192:384]),
+        bc_sum,
+        wdt_sum,
+        joined(lists[0].reshape(8, KER, chans)),
+        sums[2].reshape(KER, 2 * state),
+        lists[1].reshape(-1),
+        sums[3],
+        lists[3].reshape(-1),
+        lists[4].reshape(-1),
+        lists[5].reshape(-1),
+        lists[2].reshape(-1),
+        joined(main[:, :, 512:704]).T,
+        sums[1],
+        router_sum,
+        joined(main[:, :, 384:448]),
+        joined(main[:, :, 448:512]),
+        joined(main[:, :, 704:768]).T,
+        (grad_up[:, :256] + other[2].astype(f32))[None],
+        (grad_up[:, wide : wide + 256] + other[3].astype(f32))[None],
+        (grad_down[:256] + other[4].astype(f32))[None],
+    )
+
+
 def solution(mesh):
+    places = mesh.shape["seq"]
+    whole_heads = places == 16 and mesh.shape["head"] == 2
     placed = (
         P("seq", None, None),
         P("seq", None),
@@ -535,7 +1561,7 @@
         P("seq", None, None),
     )
     return jax.shard_map(
-        on_device,
+        by_heads if whole_heads else on_device,
         mesh=mesh,
         in_specs=placed,
         out_specs=(

time: 2770 us -> 676 us (0.24)
  waiting for transfers between devices: 1930 us -> 0 us
  blocking collectives: 385 us -> 0 us
  Pallas kernels: 0 us -> 374 us
  other arithmetic: 120 us -> 47.6 us
  matrix products: 143 us -> 95.6 us
    reduce_scatter x7 -> x0, waiting for transfers between devices: 1010 us -> none  [the longest x1 178 us: on_device(): lax.psum_scatter(grad_out_w, 'seq', scatter_dimension=1, tiled=True)]
    all_gather x8 -> x0, waiting for transfers between devices: 556 us -> none  [the longest x2 247 us: entering(): lax.all_gather(part.astype(kind), axis)]
    pallas_call x0 -> x10, Pallas kernels: none -> 374 us  [the longest x4 123 us: reduce_rows(): pl.pallas_call(functools.partial(reduce_kernel, rows), out_shape=(jax.Sha...]
    all_gather x4 -> x0, blocking collectives: 207 us -> none  [the longest x1 119 us: on_device(): lax.all_gather(router, 'seq', axis=0, tiled=True)]
    unnamed x23 -> x0, waiting for transfers between devices: 181 us -> none
    all_to_all x3 -> x0, waiting for transfers between devices: 120 us -> none  [the longest x1 120 us: on_device(): lax.all_to_all(send_grads, 'seq', split_axis=0, concat_axis=0, tiled=True)]
    all_to_all x1 -> x0, blocking collectives: 109 us -> none  [on_device(): lax.all_to_all(send_rows, 'seq', split_axis=0, concat_axis=0, tiled=True)]
    psum x4 -> x0, blocking collectives: 68.9 us -> none  [the longest x1 51 us: on_device(): lax.psum((grad_norm1, grad_norm2, grad_cweight, grad_cshift, grad_dtb, gr...]
  transfers between devices with their start and end apart: 27 -> 0, of which waited for: 22 -> 0; matrix products, arithmetic and copies ran while one was open for 7% -> 0% of each run, Pallas kernels for 0% -> 0%
where the time goes in v1:
time: 676 us; the launch traced here: 669 us
  Pallas kernels  374 us (55%)
  local copies, waits for them, and re-layouts  148 us (22%)
  matrix products  95.6 us (14%)
  other arithmetic  47.6 us (7%)
    pallas_call x4, Pallas kernels, reduce_rows(): pl.pallas_call(functools.partial(reduce_kernel, rows), out_shape=(jax.Sha...  123 us
    pallas_call x3, Pallas kernels, gather_rows(): pl.pallas_call(functools.partial(gather_kernel, rows), out_shape=(jax.Sha...  100 us
    pallas_call x1, Pallas kernels, enter(): pl.pallas_call(functools.partial(enter_kernel, rows), out_shape=(shape((1...  64.5 us
    pallas_call x1, Pallas kernels, leave(): pl.pallas_call(leave_kernel, out_shape=(shape((8,) + main.shape[1:], low)...  64 us
    unnamed x408, local copies, waits for them, and re-layouts  28 us
    dot_general x5, matrix products, flat_dot(): jnp.dot(left_side.reshape(-1, left_side.shape[-1]), right_side, preferred...  23.9 us
    pallas_call x1, Pallas kernels, swap(): pl.pallas_call(functools.partial(swap_kernel, count), out_shape=tuple((ja...  22.2 us
    dot_general x5, matrix products, flat_dot_t(): lax.dot_general(left_side.reshape(-1, left_side.shape[-1]), right_side, (...  19.1 us

profile of v1, /device:TPU:15, one launch (start us, length us, event | category | flops | bytes accessed | tf_op | source)
XLA Modules:
  0.0 668.6 jit_solution(6025682177234405186)
XLA Ops:
  11.8 3.5 concatenate.79
  15.6 64.5 %enter.1 = (bf16[1280,1536]{1,0:T(8,128)(2,1)}, bf16[256,1536]{1,0:T(8,128)(2,1)S(1)}, bf16[1536,768]{1,0:T(8,128)(2,1)}, f32[8,1536]{1,0:T(8,128)S(1)}, bf16[15...) custom-call(bf16[80,1536]{1,0:T(8,128)(2,1)S(1)} %concatenate.78.own_ref, ...), custom_call_target="tpu_custom_call" | custom-call | tf_op jit(solution)/shard_map/enter/pallas_call | solution.py:928
  80.2 4.6 slice.430
  99.0 3.8 fusion.5
  125.8 3.3 fusion.150
  130.4 4.8 fusion.26
  140.2 38.3 %reduce_2.1 = (f32[64,1536]{1,0:T(8,128)S(1)}, f32[16,8,128]{2,1,0:T(8,128)S(1)}) custom-call(bf16[1024,1536]{1,0:T(8,128)(2,1)S(1)} %convolution_convert_fusion.1.part_ref, f32[16,8,128]{2,1,0:T(8,128)S(1)} %pad.115.note_ref), custom_call_target="tpu_custom_call" | custom-call | tf_op jit(solution)/shard_map/reduce_2/pallas_call | solution.py:772
  182.2 6.6 concatenate.86
  189.0 34.1 %gather_3.1 = (bf16[1024,1536]{1,0:T(8,128)(2,1)S(1)}, f32[16,8,128]{2,1,0:T(8,128)S(1)}) custom-call(bf16[64,1536]{1,0:T(8,128)(2,1)S(1)} %multiply_convert_fusion.7.own_ref, f32[8,128]{1,0:T(8,128)S(1)} %pad.116.note_ref), custom_call_target="tpu_custom_call" | custom-call | tf_op jit(solution)/shard_map/gather_3/pallas_call | solution.py:648
  223.1 9.0 %fusion.152 = f32[1024,1152]{1,0:T(8,128)} fusion(bf16[1024,1536]{1,0:T(8,128)(2,1)S(1)} %get-tuple-element.56, bf16[1536,1152]{1,0:T(8,128)(2,1)} %concatenate.86), kind=kOutput, calls=%fused_computation.357 | convolution fusion | flops 3623878656 | bytes 11403264 | tf_op jit(solution)/shard_map/dot_general | solution.py:118
  242.9 38.1 %gather_4.1 = (bf16[1024,1536]{1,0:T(8,128)(2,1)S(1)}, f32[16,8,128]{2,1,0:T(8,128)}) custom-call(bf16[64,1536]{1,0:T(8,128)(2,1)S(1)} %bitcast.350, f32[8,128]{1,0:T(8,128)S(1)} %pad.116.note_ref), custom_call_target="tpu_custom_call" | custom-call | tf_op jit(solution)/shard_map/gather_4/pallas_call | solution.py:648
  281.0 4.7 copy.553
  286.6 6.8 %multiply_convert_fusion.1 = (bf16[1024,576]{1,0:T(8,128)(2,1)S(1)}, bf16[1024,576]{1,0:T(8,128)(2,1)S(1)}, f32[1024,576]{1,0:T(8,128)S(1)}, f32[1024,576]{1,0:T(8,128)S(1)}) fusion(f32[1024,1152]{1,0:T(8,128)} %fusion.152, f32[1024,512]{1,0:T(8,128)} %broadcast_in_dim.77, bf16[1024,1536]{1,0:T(8,128)(2,1)S(1)} %get-tuple-element.61, ...), kind=kOutput, calls=%fused_computation.9 | convolution fusion | flops 1826684928 | bytes 18808832 | tf_op jit(solution)/shard_map/dot_general | solution.py:126
  293.5 4.9 convolution_convert_fusion.3.part_ref
  298.8 26.7 %reduce_6.1 = (f32[64,1536]{1,0:T(8,128)S(1)}, f32[16,8,128]{2,1,0:T(8,128)S(1)}) custom-call(bf16[1024,1536]{1,0:T(8,128)(2,1)S(1)} %convolution_convert_fusion.3.part_ref, f32[16,8,128]{2,1,0:T(8,128)S(1)} %pad.119.note_ref), custom_call_target="tpu_custom_call" | custom-call | tf_op jit(solution)/shard_map/reduce_6/pallas_call | solution.py:772
  330.0 5.4 convolution_convert_fusion.part_ref
  335.5 26.8 %reduce_5.1 = (f32[64,1536]{1,0:T(8,128)S(1)}, f32[16,8,128]{2,1,0:T(8,128)}) custom-call(bf16[1024,1536]{1,0:T(8,128)(2,1)S(1)} %convolution_convert_fusion.part_ref, f32[16,8,128]{2,1,0:T(8,128)S(1)} %pad.118.note_ref), custom_call_target="tpu_custom_call" | custom-call | tf_op jit(solution)/shard_map/reduce_5/pallas_call | solution.py:772
  363.5 28.2 %gather_7.1 = (bf16[1024,1536]{1,0:T(8,128)(2,1)S(1)}, f32[16,8,128]{2,1,0:T(8,128)S(1)}) custom-call(bf16[64,1536]{1,0:T(8,128)(2,1)S(1)} %get-tuple-element.285.own_ref, f32[8,128]{1,0:T(8,128)S(1)} %pad.120.note_ref), custom_call_target="tpu_custom_call" | custom-call | tf_op jit(solution)/shard_map/gather_7/pallas_call | solution.py:648
  392.0 5.2 multiply_reduce_fusion.7
  397.4 5.2 fusion.31
  420.0 3.3 convolution_bitcast_fusion
  426.8 3.3 convolution_bitcast_fusion.1
  434.1 4.0 fusion.23
  440.2 3.6 multiply_reduce_fusion.2
  450.0 31.0 %reduce_8.1 = (f32[64,1536]{1,0:T(8,128)S(1)}, f32[16,8,128]{2,1,0:T(8,128)}) custom-call(bf16[1024,1536]{1,0:T(8,128)(2,1)S(1)} %convolution_convert_fusion.2.part_ref, f32[16,8,128]{2,1,0:T(8,128)S(1)} %pad.118.note_ref), custom_call_target="tpu_custom_call" | custom-call | tf_op jit(solution)/shard_map/reduce_8/pallas_call | solution.py:772
  482.1 8.2 %fusion.145 = (bf16[1536,1152]{1,0:T(8,128)(2,1)S(1)}, f32[1536,1152]{1,0:T(8,128)}) fusion(bf16[1024,1536]{1,0:T(8,128)(2,1)S(1)} %copy-done.3, bf16[1024,576]{1,0:T(8,128)(2,1)} %copy-done.190, bf16[1024,576]{1,0:T(8,128)(2,1)S(1)} %copy-done.189), kind=kOutput, calls=%fused_computation.350 | convolution fusion | flops 3630366720 | bytes 16121856 | tf_op jit(solution)/shard_map/dot_general | solution.py:136
  494.0 4.0 fusion.146
  500.1 22.2 %swap_10.1 = (f32[64,1536]{1,0:T(8,128)}, f32[64,1536]{1,0:T(8,128)}, bf16[1536,256]{1,0:T(8,128)(2,1)}, bf16[1536,256]{1,0:T(8,128)(2,1)}, bf16[256,1536]{1,0:T(8,128)(2,1)}) custom-call(f32[64,1536]{1,0:T(8,128)} %get-tuple-element.333.refs_0_, f32[64,1536]{1,0:T(8,128)} %fusion.74.refs_1_, bf16[1536,256]{1,0:T(8,128)(2,1)} %get-tuple-element.310.refs_2_, ...), custom_call_target="tpu_custom_call" | custom-call | tf_op jit(solution)/shard_map/swap_10/pallas_call | solution.py:1155
  527.6 4.1 fusion.147
  554.8 64.0 %leave.1 = (bf16[8,96,768]{2,1,0:T(8,128)(2,1)}, f32[112,256]{1,0:T(8,128)}, f32[16,88,128]{2,1,0:T(8,128)}) custom-call(bf16[16,96,768]{2,1,0:T(8,128)(2,1)} %concatenate.97.main_ref, bf16[16,112,256]{2,1,0:T(8,128)(2,1)} %maximum_maximum_fusion.bcr_ref, f32[88,128]{1,0:T(8,128)} %pad_bitcast_fusion.small_ref), custom_call_target="tpu_custom_call" | custom-call | tf_op jit(solution)/shard_map/leave/pallas_call | solution.py:1106
  634.3 4.6 reshape.577
  661.0 4.4 fusion.7
  (645 shorter events, 183.4 us)
Async XLA Ops:
  98.6 16.5 %copy-start.25 = (s32[1024,7]{1,0:T(8,128)}, s32[1024,7]{1,0:T(8,128)S(1)}, u32[]{:S(2)}) copy-start(s32[1024,7]{1,0:T(8,128)S(1)} %reshape.592) | copy-start | bytes 86020
  99.0 38.6 %copy-start.149 = (f32[1,192]{1,0:T(1,128)}, f32[1,192]{1,0:T(1,128)S(1)}, u32[]{:S(2)}) copy-start(f32[1,192]{1,0:T(1,128)S(1)} %get-tuple-element.334) | copy-start | bytes 2308
  103.1 7.4 %copy-start.165 = (f32[3]{0:T(128)}, f32[3]{0:T(128)S(1)}, u32[]{:S(2)}) copy-start(f32[3]{0:T(128)S(1)} %get-tuple-element.353) | copy-start | bytes 40
  103.3 32.4 %copy-start.147 = (f32[192]{0:T(256)}, f32[192]{0:T(256)S(1)}, u32[]{:S(2)}) copy-start(f32[192]{0:T(256)S(1)} %mul.903) | copy-start | bytes 2308
  109.6 20.8 %copy-start.33 = (f32[24,8,8,128]{3,2,1,0:T(8,128)}, f32[24,8,8,128]{3,2,1,0:T(8,128)S(1)}, u32[]{:S(2)}) copy-start(f32[24,8,8,128]{3,2,1,0:T(8,128)S(1)} %copy.640) | copy-start | bytes 2359300
  122.6 7.8 %copy-start.138 = (f32[8,3,128]{2,1,0:T(4,128)}, f32[8,3,128]{2,1,0:T(4,128)S(1)}, u32[]{:S(2)}) copy-start(f32[8,3,128]{2,1,0:T(4,128)S(1)} %copy.540) | copy-start | bytes 36868
  140.1 39.2 %copy-start.43 = (bf16[64,1536]{1,0:T(8,128)(2,1)S(1)}, bf16[64,1536]{1,0:T(8,128)(2,1)}, u32[]{:S(2)}) copy-start(bf16[64,1536]{1,0:T(8,128)(2,1)} %copy-done.42) | copy-start | bytes 589828
  179.5 9.3 %copy-start.39 = (f32[64,1536]{1,0:T(8,128)}, f32[64,1536]{1,0:T(8,128)S(1)}, u32[]{:S(2)}) copy-start(f32[64,1536]{1,0:T(8,128)S(1)} %get-tuple-element.288) | copy-start | bytes 1179652
  180.1 8.7 %copy-start.167 = (f32[64]{0:T(128)}, f32[64]{0:T(128)S(1)}, u32[]{:S(2)}) copy-start(f32[64]{0:T(128)S(1)} %get-tuple-element.357) | copy-start | bytes 772
  223.1 16.2 %copy-start.2 = (bf16[1024,1536]{1,0:T(8,128)(2,1)}, bf16[1024,1536]{1,0:T(8,128)(2,1)S(1)}, u32[]{:S(2)}) copy-start(bf16[1024,1536]{1,0:T(8,128)(2,1)S(1)} %get-tuple-element.56) | copy-start | bytes 9437188
  223.1 9.0 %copy-start.26 = (s32[1024,7]{1,0:T(8,128)S(1)}, s32[1024,7]{1,0:T(8,128)}, u32[]{:S(2)}) copy-start(s32[1024,7]{1,0:T(8,128)} %copy-done.25) | copy-start | bytes 86020
  286.6 6.9 %copy-start.94 = (bf16[64,1536]{1,0:T(8,128)(2,1)}, bf16[64,1536]{1,0:T(8,128)(2,1)S(1)}, u32[]{:S(2)}) copy-start(bf16[64,1536]{1,0:T(8,128)(2,1)S(1)} %slice_bitcast_fusion.10) | copy-start | bytes 589828
  286.6 6.9 %copy-start.56 = (bf16[1536,1152]{1,0:T(8,128)(2,1)S(1)}, bf16[1536,1152]{1,0:T(8,128)(2,1)}, u32[]{:S(2)}) copy-start(bf16[1536,1152]{1,0:T(8,128)(2,1)} %concatenate.86) | copy-start | bytes 10616836
  298.7 29.1 %copy-start.168 = (f32[64]{0:T(128)S(1)}, f32[64]{0:T(128)}, u32[]{:S(2)}) copy-start(f32[64]{0:T(128)} %copy-done.167) | copy-start | bytes 772
  327.8 7.6 %copy-start.121 = (bf16[64,16]{0,1:T(8,128)(2,1)}, bf16[64,16]{0,1:T(8,128)(2,1)S(1)}, u32[]{:S(2)}) copy-start(bf16[64,16]{0,1:T(8,128)(2,1)S(1)} %multiply_convert_fusion.8) | copy-start | bytes 6148
  335.4 26.9 %copy-start.11 = (f32[64,1536]{1,0:T(8,128)S(1)}, f32[64,1536]{1,0:T(8,128)}, u32[]{:S(2)}) copy-start(f32[64,1536]{1,0:T(8,128)} %copy-done.10) | copy-start | bytes 1179652
  335.4 26.9 %copy-start.40 = (f32[64,1536]{1,0:T(8,128)S(1)}, f32[64,1536]{1,0:T(8,128)}, u32[]{:S(2)}) copy-start(f32[64,1536]{1,0:T(8,128)} %copy-done.39) | copy-start | bytes 1179652
  335.4 26.9 %copy-start.59 = (bf16[64,1,1536]{2,1,0:T(2,128)(2,1)S(1)}, bf16[64,1,1536]{2,1,0:T(2,128)(2,1)}, u32[]{:S(2)}) copy-start(bf16[64,1,1536]{2,1,0:T(2,128)(2,1)} %get-tuple-element.370) | copy-start | bytes 589828
  335.4 26.9 %copy-start.173 = (f32[64]{0:T(128)S(1)}, f32[64]{0:T(128)}, u32[]{:S(2)}) copy-start(f32[64]{0:T(128)} %copy-done.172) | copy-start | bytes 772
  335.4 26.9 %copy-start.185 = (f32[64]{0:T(128)S(1)}, f32[64]{0:T(128)}, u32[]{:S(2)}) copy-start(f32[64]{0:T(128)} %get-tuple-element.356) | copy-start | bytes 772
  409.7 7.2 %copy-start.166 = (f32[3]{0:T(128)S(1)}, f32[3]{0:T(128)}, u32[]{:S(2)}) copy-start(f32[3]{0:T(128)} %copy-done.165) | copy-start | bytes 40
  409.7 8.1 %copy-start.164 = (f32[3]{0:T(128)S(1)}, f32[3]{0:T(128)}, u32[]{:S(2)}) copy-start(f32[3]{0:T(128)} %copy-done.163) | copy-start | bytes 40
  447.2 33.8 %copy-start.44 = (bf16[64,1536]{1,0:T(8,128)(2,1)S(1)}, bf16[64,1536]{1,0:T(8,128)(2,1)}, u32[]{:S(2)}) copy-start(bf16[64,1536]{1,0:T(8,128)(2,1)} %copy-done.42) | copy-start | bytes 589828
  447.2 33.8 %copy-start.112 = (f32[1536]{0:T(1024)S(1)}, f32[1536]{0:T(1024)}, u32[]{:S(2)}) copy-start(f32[1536]{0:T(1024)} %param.29) | copy-start | bytes 18436
  447.2 33.8 %copy-start.162 = (f32[64]{0:T(128)S(1)}, f32[64]{0:T(128)}, u32[]{:S(2)}) copy-start(f32[64]{0:T(128)} %copy-done.161) | copy-start | bytes 772
  449.9 31.2 %copy-start.72 = (f32[64,1536]{1,0:T(8,128)S(1)}, f32[64,1536]{1,0:T(8,128)}, u32[]{:S(2)}) copy-start(f32[64,1536]{1,0:T(8,128)} %get-tuple-element.286) | copy-start | bytes 1179652
  449.9 31.2 %copy-start.178 = (f32[64]{0:T(128)S(1)}, f32[64]{0:T(128)}, u32[]{:S(2)}) copy-start(f32[64]{0:T(128)} %get-tuple-element.354) | copy-start | bytes 772
  450.0 32.1 %copy-start.3 = (bf16[1024,1536]{1,0:T(8,128)(2,1)S(1)}, bf16[1024,1536]{1,0:T(8,128)(2,1)}, u32[]{:S(2)}) copy-start(bf16[1024,1536]{1,0:T(8,128)(2,1)} %copy-done.2) | copy-start | bytes 9437188
  450.0 32.1 %copy-start.189 = (bf16[1024,576]{1,0:T(8,128)(2,1)S(1)}, bf16[1024,576]{1,0:T(8,128)(2,1)}, u32[]{:S(2)}) copy-start(bf16[1024,576]{1,0:T(8,128)(2,1)} %copy-done.188) | copy-start | bytes 3538948
  482.1 10.8 %copy-start.24 = (f32[1024,576]{1,0:T(8,128)S(1)}, f32[1024,576]{1,0:T(8,128)}, u32[]{:S(2)}) copy-start(f32[1024,576]{1,0:T(8,128)} %copy-done.23) | copy-start | bytes 7077892
  482.1 10.8 %copy-start.27 = (f32[1024,512]{1,0:T(8,128)S(1)}, f32[1024,512]{1,0:T(8,128)}, u32[]{:S(2)}) copy-start(f32[1024,512]{1,0:T(8,128)} %broadcast_in_dim.77) | copy-start | bytes 6291460
  623.7 6.9 %copy-start.98 = (f32[112,256]{1,0:T(8,128)S(1)}, f32[112,256]{1,0:T(8,128)}, u32[]{:S(2)}) copy-start(f32[112,256]{1,0:T(8,128)} %get-tuple-element.72) | copy-start | bytes 344068
  (160 other events, 550.1 us)

commit v2 on v1

--- a/solution.py
+++ b/solution.py
@@ -567,7 +567,7 @@
     return ref.at[pl.ds(pl.multiple_of(start, step), size)]
 
 
-def gather_steps(mail, own_ref, out_ref, recv, recv_half, rows, half):
+def gather_steps(mail, own_ref, out_ref, recv, recv_half, rows, half=None):
     here, side, z, col, cx, cy, cd = peers()
     zs = layers(z)
     base = 4 * z
@@ -576,6 +576,10 @@
         return rows_at(out_ref, place * rows, rows, 16)
 
     def part(place, which):
+        if half is None:
+            width = out_ref.shape[1] // 2
+            at = pl.ds(pl.multiple_of(place * rows, 16), rows)
+            return out_ref.at[at, pl.ds(which * width, width)]
         size = rows - half if which else half
         return rows_at(out_ref, place * rows + which * half, size, 16)
 
@@ -751,58 +755,20 @@
     return [VMEM(shape + (width,), kind) for shape in shapes]
 
 
-def reduce_kernel(rows, part_ref, note_ref, out_ref, notes_out, *refs):
-    got, sums, (send, recv, recv_n) = refs[:5], refs[5:8], refs[8:]
-    here, side = peers()[:2]
-    greet(same_side(side, here))
-    mail = Mail(send)
-    steps = reduce_steps(mail, part_ref, out_ref, got, sums, recv, rows)
-    next(steps)
-    notes_out[here] = note_ref[here]
-    note_puts(mail, lambda to: note_ref.at[to], notes_out, recv_n)
-    for _ in steps:
-        pass
-    note_waits(mail, notes_out, recv_n)
-    mail.finish()
-
-
-def reduce_rows(parts, notes, number):
-    rows, width = parts.shape[0] // 16, parts.shape[1]
-    vmem = pl.BlockSpec(memory_space=VMEM)
-    return pl.pallas_call(
-        functools.partial(reduce_kernel, rows),
-        out_shape=(
-            jax.ShapeDtypeStruct((rows, width), jnp.float32),
-            jax.ShapeDtypeStruct(notes.shape, notes.dtype),
-        ),
-        in_specs=[vmem, vmem],
-        out_specs=(vmem, vmem),
-        scratch_shapes=reduce_scratch(rows, width, parts.dtype)
-        + [
-            pltpu.SemaphoreType.DMA((42,)),
-            pltpu.SemaphoreType.DMA((27,)),
-            pltpu.SemaphoreType.DMA((16,)),
-        ],
-        compiler_params=pltpu.CompilerParams(
-            collective_id=number, has_side_effects=True, vmem_limit_bytes=48 << 20
-        ),
-        name=f"reduce_{number}",
-    )(parts, notes)
-
-
 def same_side(side, here):
     return [(lax.rem(here + k, 16), side) for k in range(1, 16)]
 
 
 def enter_kernel(
-    rows,
     own_ref,
+    mine_ref,
     blocks_ref,
     small_ref,
     gate_ref,
     up_ref,
     down_ref,
     all_ref,
+    extras_ref,
     extra_ref,
     cols_ref,
     small_other,
@@ -812,6 +778,8 @@
     send,
     recv,
     recv_half,
+    recv_m,
+    recv_half_m,
     recv_w,
     recv_e,
     recv_s,
@@ -822,22 +790,24 @@
     sibling = (here, 1 - side)
     greet(same_side(side, here) + [sibling])
     depth = blocks_ref.shape[1]
-    extra = rows - 64
+    rows, extra = own_ref.shape[0], mine_ref.shape[0]
     half_here = here // 8
     mail = Mail(send)
     mine = pltpu.make_async_copy(own_ref, rows_at(all_ref, here * rows, rows, 16), local.at[0])
     mine.start()
+    mine_too = pltpu.make_async_copy(
+        mine_ref, rows_at(extras_ref, here * extra, extra, 16), local.at[18]
+    )
+    mine_too.start()
 
     def strip(place):
         return rows_at(cols_ref, place * depth, depth, 16)
 
-    steps = gather_steps(mail, own_ref, all_ref, recv, recv_half, rows, rows // 32 * 16)
+    steps = gather_steps(mail, own_ref, all_ref, recv, recv_half, rows, rows // 2)
+    steps_too = gather_steps(mail, mine_ref, extras_ref, recv_m, recv_half_m, extra)
+    next(steps_too)
     next(steps)
     mail.put(small_ref, small_other, recv_s.at[0], sibling)
-    away = []
-    for k in range(1, 8):
-        to = 8 * side + lax.rem(here + k, 8)
-        away.append(to)
     first = 8 * side + lax.rem(here, 8)
     is_mine = side == half_here
     for k in range(1, 8):
@@ -862,12 +832,15 @@
     mail.put(gate_ref, gate_other, recv_s.at[1], sibling)
     mail.put(up_ref, up_other, recv_s.at[2], sibling)
     mail.put(down_ref, down_other, recv_s.at[3], sibling)
+    for _ in steps_too:
+        next(steps)
     for _ in steps:
         pass
     mine.wait()
+    mine_too.wait()
     for place in range(places):
-        src = all_ref.at[pl.ds(place * rows + 64, extra)]
-        mail.put(src, extra_ref.at[pl.ds(place * extra, extra)], recv_e.at[place], sibling)
+        at = pl.ds(place * extra, extra)
+        mail.put(extras_ref.at[at], extra_ref.at[at], recv_e.at[place], sibling)
 
     def forward(place, sem):
         return pltpu.make_async_remote_copy(
@@ -918,17 +891,18 @@
     mail.finish()
 
 
-def enter(own, blocks, small, gate, up, down, number):
+def enter(own, mine, blocks, small, gate, up, down, number):
     rows, width = own.shape
-    extra = rows - 64
+    extra = mine.shape[0]
     depth, cols = blocks.shape[1:]
     shape = jax.ShapeDtypeStruct
     hbm = pl.BlockSpec(memory_space=pl.ANY)
     vmem = pl.BlockSpec(memory_space=VMEM)
     return pl.pallas_call(
-        functools.partial(enter_kernel, rows),
+        enter_kernel,
         out_shape=(
             shape((16 * rows, width), own.dtype),
+            shape((16 * extra, width), own.dtype),
             shape((16 * extra, width), own.dtype),
             shape((16 * depth, cols), blocks.dtype),
             shape(small.shape, small.dtype),
@@ -936,22 +910,24 @@
             shape(up.shape, up.dtype),
             shape(down.shape, down.dtype),
         ),
-        in_specs=[vmem, vmem, vmem, hbm, hbm, hbm],
-        out_specs=(vmem, vmem, vmem, vmem, hbm, hbm, hbm),
+        in_specs=[vmem, vmem, vmem, vmem, hbm, hbm, hbm],
+        out_specs=(vmem, vmem, vmem, vmem, vmem, hbm, hbm, hbm),
         scratch_shapes=[
-            pltpu.SemaphoreType.DMA((46,)),
+            pltpu.SemaphoreType.DMA((65,)),
+            pltpu.SemaphoreType.DMA((11,)),
+            pltpu.SemaphoreType.DMA((8,)),
             pltpu.SemaphoreType.DMA((11,)),
             pltpu.SemaphoreType.DMA((8,)),
             pltpu.SemaphoreType.DMA((16,)),
             pltpu.SemaphoreType.DMA((16,)),
             pltpu.SemaphoreType.DMA((4,)),
-            pltpu.SemaphoreType.DMA((18,)),
+            pltpu.SemaphoreType.DMA((19,)),
         ],
         compiler_params=pltpu.CompilerParams(
             collective_id=number, has_side_effects=True, vmem_limit_bytes=48 << 20
         ),
         name="enter",
-    )(own, blocks, small, gate, up, down)
+    )(own, mine, blocks, small, gate, up, down)
 
 
 def leave_kernel(
@@ -1166,38 +1142,601 @@
     )(*arrays)
 
 
-def chunked(array, chunk):
-    return array.reshape((array.shape[0] // chunk, chunk) + array.shape[1:])
-
-
-def scan_core(x_heads, step_size, b_state, c_state, decay_rate, doc_ids, chunk):
-    length = doc_ids.shape[0]
-    prev_all = jnp.concatenate([doc_ids[:1], doc_ids[:-1]], 0)
-    docs, prev = chunked(doc_ids, chunk), chunked(prev_all, chunk)[:, :1]
-    x_c, step_c = chunked(x_heads, chunk), chunked(step_size, chunk)
-    b_c, c_c = chunked(b_state, chunk), chunked(c_state, chunk)
-    logs = jnp.cumsum(step_c * decay_rate, axis=1)
-    causal = jnp.arange(chunk)[:, None] >= jnp.arange(chunk)[None, :]
-    pair = causal[None] & (docs[:, :, None] == docs[:, None, :])
-    logs_h = logs.transpose(0, 2, 1)
-    gap = logs_h[:, :, :, None] - logs_h[:, :, None, :]
-    table = jnp.exp(jnp.where(pair[:, None], gap, 0.0)) * pair[:, None].astype(jnp.float32)
-    cross = jnp.einsum("gtn,gun->gtu", c_c, b_c, precision=HIGH)
-    weights = table * cross[:, None] * step_c.transpose(0, 2, 1)[:, :, None, :]
-    intra = jnp.einsum("ghtu,guhp->gthp", weights, x_c, precision=HIGH)
-    enters = jnp.exp(logs) * (docs == prev).astype(jnp.float32)[..., None]
-    end_keep = (docs == docs[:, -1:]).astype(jnp.float32)
-    tail = jnp.exp(logs[:, -1:] - logs) * end_keep[..., None] * step_c
-    local = jnp.einsum("gth,gthp,gtn->ghpn", tail, x_c, b_c, precision=HIGH)
-    keep = enters[:, -1]
-    state = jnp.zeros_like(local[0])
-    before = []
-    for group in range(length // chunk):
-        before.append(state)
-        state = keep[group][:, None, None] * state + local[group]
-    before = jnp.stack(before)
-    inter = jnp.einsum("gtn,ghpn->gthp", c_c, before, precision=HIGH) * enters[..., None]
-    return (intra + inter).reshape(x_heads.shape)
+CHUNK = 128
+LAYER = 256
+HEADW = 64
+
+
+def mm(left, right, low=True, exact=False):
+    return mm_of(left, right, ((1,), (0,)), low, exact)
+
+
+def mm_nt(left, right, low=True, exact=False):
+    return mm_of(left, right, ((1,), (1,)), low, exact)
+
+
+def mm_tn(left, right, low=True, exact=False):
+    return mm_of(left, right, ((0,), (0,)), low, exact)
+
+
+def mm_of(left, right, dims, low, exact):
+    if exact:
+        return lax.dot_general(
+            left, right, (dims, ((), ())), precision=HIGH, preferred_element_type=jnp.float32
+        )
+    if low:
+        left, right = left.astype(jnp.bfloat16), right.astype(jnp.bfloat16)
+    return lax.dot_general(left, right, (dims, ((), ())), preferred_element_type=jnp.float32)
+
+
+def lanes(shape):
+    return lax.broadcasted_iota(jnp.int32, shape, 1)
+
+
+def by_head(parts, rows):
+    lane = lanes((rows, 3 * HEADW))
+    return jnp.where(lane < HEADW, parts[0], jnp.where(lane < 2 * HEADW, parts[1], parts[2]))
+
+
+def spread_heads(array):
+    return by_head([array[:, h : h + 1] for h in range(3)], array.shape[0])
+
+
+def soft_plus(values):
+    return jnp.maximum(values, 0.0) + jnp.log1p(jnp.exp(-jnp.abs(values)))
+
+
+def chunk_tables(step, log_rate, doc_col, doc_row):
+    row = lax.broadcasted_iota(jnp.int32, (CHUNK, CHUNK), 0)
+    col = lax.broadcasted_iota(jnp.int32, (CHUNK, CHUNK), 1)
+    below = (row >= col).astype(jnp.float32)
+    logs = mm(below, step * log_rate, exact=True)
+    logs_t, step_t = logs.T, step.T
+    pair = (row >= col) & (doc_col == doc_row)
+    tables = [
+        jnp.exp(jnp.where(pair, logs[:, h : h + 1] - logs_t[h : h + 1], -1e9)) for h in range(3)
+    ]
+    return logs, tables, [step_t[h : h + 1] for h in range(3)]
+
+
+def mix_forward_kernel(
+    n1_ref,
+    cols_ref,
+    wbc_ref,
+    wdt_ref,
+    taps_ref,
+    head_ref,
+    gain_ref,
+    info_ref,
+    docrow_ref,
+    g_ref,
+    z_ref,
+    ext_ref,
+    pre_ref,
+    dt_ref,
+    y_ref,
+    state_ref,
+    out_ref,
+    notes_out,
+    g_all_ref,
+    part_ref,
+    gained_ref,
+    notes_ref,
+    *refs,
+):
+    got, sums, refs = refs[:5], refs[5:8], refs[8:]
+    send, recv, recv_n, g_send, g_recv, g_recv_half, local = refs
+    here, side, z_at = peers()[:3]
+    greet(same_side(side, here))
+    low, f32 = jnp.bfloat16, jnp.float32
+    mine = pltpu.make_async_copy(g_ref, rows_at(g_all_ref, here * 64, 64, 16), local)
+    mine.start()
+    g_mail = Mail(g_send)
+    g_steps = gather_steps(g_mail, g_ref, g_all_ref, g_recv, g_recv_half, 64, 32)
+    next(g_steps)
+
+    ext_ref[0:8] = jnp.zeros((8, ext_ref.shape[1]), f32)
+
+    @pl.loop(0, 4)
+    def _(i):
+        at = pl.ds(pl.multiple_of(i * LAYER, LAYER), LAYER)
+        shifted = pl.ds(pl.multiple_of(i * LAYER + 8, 8), LAYER)
+        rows = n1_ref[at]
+        z_ref[at] = mm(rows, cols_ref[:, 0:192])
+        ext_ref[shifted, 0:256] = mm(rows, wbc_ref[...])
+        ext_ref[shifted, 256:448] = mm(rows, cols_ref[:, 256:448])
+        dt_ref[at] = mm(rows, wdt_ref[...]) + head_ref[0:1]
+
+    next(g_steps)
+    rate, skip = head_ref[1:2], spread_heads(head_ref[2:3])
+    state = jnp.zeros((128, 192), f32)
+    ones = jnp.ones((8, 192), f32)
+    for c in range(8):
+        r = c * CHUNK
+        at = pl.ds(r, CHUNK)
+        info = info_ref[at]
+        pre = taps_ref[4:5] + taps_ref[3:4] * ext_ref[pl.ds(r + 8, CHUNK)]
+        for k in (1, 2, 3):
+            pre = pre + taps_ref[3 - k : 4 - k] * ext_ref[pl.ds(r + 8 - k, CHUNK)] * (
+                info[:, k - 1 : k]
+            )
+        pre_ref[at] = pre
+        act = pre * jax.nn.sigmoid(pre)
+        b, cc, x = act[:, 0:128], act[:, 128:256], act[:, 256:448]
+        step = soft_plus(dt_ref[at])
+        logs, tables, step_t = chunk_tables(step, rate, info[:, 3:4], docrow_ref[0:1, at])
+        cross = mm_nt(cc, b)
+        stacked = jnp.concatenate([cross * tables[h] * step_t[h] for h in range(3)], 0)
+        intra = mm(stacked, x)
+        y = by_head([intra[h * CHUNK : (h + 1) * CHUNK] for h in range(3)], CHUNK)
+        enters = jnp.exp(logs) * info[:, 4:5]
+        state_ref[c] = state
+        y = y + spread_heads(enters) * mm(cc, state) + skip * x
+        y_ref[at] = y
+        tail = jnp.exp(logs[CHUNK - 1 :] - logs) * info[:, 5:6] * step
+        state = spread_heads(enters[CHUNK - 1 :]) * state + mm_tn(b, spread_heads(tail) * x)
+        z = z_ref[at]
+        gated = y * z * jax.nn.sigmoid(z)
+        gained_ref[at] = (gated * gain_ref[0:1]).astype(low)
+        squares = mm_nt(ones, gated * gated, exact=True)
+        notes_ref[2 * c, :, 0:64] = squares[:, 0:64]
+        notes_ref[2 * c + 1, :, 0:64] = squares[:, 64:128]
+        next(g_steps, None)
+
+    mail = Mail(send)
+    zs = layers(z_at)
+    steps = reduce_steps(mail, part_ref, out_ref, got, sums, recv, 64)
+    left = [3, 2, 1, 0]
+    for turn in range(13):
+        if turn in (0, 1, 3, 6):
+            at = pl.ds(pl.multiple_of(zs[left.pop(0)] * LAYER, LAYER), LAYER)
+            part_ref[at] = mm_nt(gained_ref[at], cols_ref[:, 512:704]).astype(low)
+        next(steps, None)
+        if turn == 0:
+            notes_out[here] = notes_ref[here]
+            note_puts(mail, lambda to: notes_ref.at[to], notes_out, recv_n)
+        if turn > 2:
+            next(g_steps, None)
+    for _ in g_steps:
+        pass
+    for _ in steps:
+        pass
+    note_waits(mail, notes_out, recv_n)
+    mine.wait()
+    g_mail.finish()
+    mail.finish()
+
+
+def mix_forward(n1, cols, wbc, wdt, taps, head, gain, info, docrow, g_own, number):
+    shape, f32, low = jax.ShapeDtypeStruct, jnp.float32, jnp.bfloat16
+    vmem = pl.BlockSpec(memory_space=VMEM)
+    dma = pltpu.SemaphoreType.DMA
+    outs = (
+        shape((1024, 192), f32),
+        shape((1032, 448), f32),
+        shape((1024, 448), f32),
+        shape((1024, 128), f32),
+        shape((1024, 192), f32),
+        shape((8, 128, 192), f32),
+        shape((64, 1536), f32),
+        shape((16, 8, 128), f32),
+        shape((1024, 1536), low),
+    )
+    return pl.pallas_call(
+        mix_forward_kernel,
+        out_shape=outs,
+        in_specs=[vmem] * 10,
+        out_specs=(vmem,) * len(outs),
+        scratch_shapes=[
+            VMEM((1024, 1536), low),
+            VMEM((1024, 192), low),
+            VMEM((16, 8, 128), f32),
+        ]
+        + reduce_scratch(64, 1536, low)
+        + [
+            dma((42,)),
+            dma((27,)),
+            dma((16,)),
+            dma((19,)),
+            dma((11,)),
+            dma((8,)),
+            dma,
+        ],
+        compiler_params=pltpu.CompilerParams(
+            collective_id=number, has_side_effects=True, vmem_limit_bytes=56 << 20
+        ),
+        name="mix_forward",
+    )(n1, cols, wbc, wdt, taps, head, gain, info, docrow, g_own)
+
+
+def moe_kernel(
+    n2_ref,
+    g_ref,
+    cols_ref,
+    eg_ref,
+    ego_ref,
+    eu_ref,
+    euo_ref,
+    ed_ref,
+    edo_ref,
+    router_ref,
+    named_ref,
+    out_ref,
+    notes_out,
+    probs_ref,
+    moe_ref,
+    gup_ref,
+    gdown_ref,
+    gsh_ref,
+    part_ref,
+    act_ref,
+    hid_ref,
+    notes_ref,
+    *refs,
+):
+    got, sums, refs = refs[:5], refs[5:8], refs[8:]
+    send, recv, recv_n = refs
+    here, side, z_at = peers()[:3]
+    greet(same_side(side, here))
+    low, f32 = jnp.bfloat16, jnp.float32
+    zs = layers(z_at)
+    ones = jnp.ones((8, 256), f32)
+    spare = lanes((LAYER, 128)) >= 64
+    pieces = (
+        (eg_ref, eu_ref, ed_ref, 0, 256),
+        (ego_ref, euo_ref, edo_ref, 256, 256),
+    )
+
+    def layer(k):
+        start = pl.multiple_of(zs[k] * LAYER, LAYER)
+        at = pl.ds(start, LAYER)
+        rows, grads = n2_ref[at], g_ref[at]
+        logits = mm(rows, router_ref[...])
+        named = named_ref[at]
+        top = jnp.max(jnp.where(named > 0, logits, -1e30), axis=-1, keepdims=True)
+        raised = jnp.exp(jnp.where(named > 0, logits - top, 0.0)) * named
+        probs = raised / jnp.sum(raised, axis=-1, keepdims=True)
+        probs_ref[at] = probs
+        prob = jnp.sum(jnp.where(lanes((LAYER, 128)) == here, probs, 0.0), axis=-1, keepdims=True)
+        dn2 = jnp.zeros((LAYER, 1536), f32)
+        slopes = jnp.zeros((8, LAYER), f32)
+        for gate_w, up_w, down_w, lane, size in pieces:
+            gate = mm(rows, gate_w[...])
+            up = mm(rows, up_w[...])
+            d_act = mm_nt(grads, down_w[...])
+            sig = jax.nn.sigmoid(gate)
+            act = gate * sig * up
+            act_ref[at, lane : lane + size] = (act * prob).astype(low)
+            slopes = slopes + mm_nt(ones, act * d_act, exact=True)
+            d_act = d_act * prob
+            d_up = (d_act * gate * sig).astype(low)
+            d_gate = (d_act * up * silu_slope(gate, sig)).astype(low)
+            hid_ref[at, lane : lane + size] = d_gate
+            hid_ref[at, 640 + lane : 640 + lane + size] = d_up
+            dn2 = dn2 + mm_nt(d_gate, gate_w[...]) + mm_nt(d_up, up_w[...])
+        gate = mm(rows, cols_ref[:, 128:256])
+        up = mm(rows, cols_ref[:, 384:512])
+        d_act = jnp.where(spare, mm(grads, cols_ref[:, 640:768]), 0.0)
+        sig = jax.nn.sigmoid(gate)
+        act_ref[at, 512:640] = jnp.where(spare, gate * sig * up, 0.0).astype(low)
+        d_up = (d_act * gate * sig).astype(low)
+        d_gate = (d_act * up * silu_slope(gate, sig)).astype(low)
+        hid_ref[at, 512:640] = d_gate
+        hid_ref[at, 1152:1280] = d_up
+        dn2 = dn2 + mm_nt(d_gate, cols_ref[:, 128:256]) + mm_nt(d_up, cols_ref[:, 384:512])
+        part_ref[at] = dn2.astype(low)
+        for j in range(4):
+            notes_ref[4 * zs[k] + j, :, 0:64] = slopes[:, 64 * j : 64 * (j + 1)]
+
+    def later(task):
+        if task < 5:
+            cols = slice(256 * task, 256 * (task + 1))
+            gup_ref[:, cols] = mm_tn(n2_ref[...], hid_ref[:, cols])
+        elif task == 5:
+            gdown_ref[...] = mm_tn(act_ref[:, 0:512], g_ref[...])
+        elif task == 6:
+            gsh_ref[...] = mm_tn(g_ref[...], act_ref[:, 512:640])
+        else:
+            at = pl.ds(256 * (task - 7), 256)
+            total = mm(act_ref[at, 0:256], ed_ref[...]) + mm(act_ref[at, 256:512], edo_ref[...])
+            total = total + mm_nt(act_ref[at, 512:640], cols_ref[:, 640:768])
+            moe_ref[at] = total.astype(low)
+
+    mail = Mail(send)
+    steps = reduce_steps(mail, part_ref, out_ref, got, sums, recv, 64)
+    left = [3, 2, 1, 0]
+    tasks = list(range(11))
+    for turn in range(13):
+        if turn in (0, 1, 3, 6):
+            layer(left.pop(0))
+        next(steps, None)
+        if turn == 6:
+            notes_out[here] = notes_ref[here]
+            note_puts(mail, lambda to: notes_ref.at[to], notes_out, recv_n)
+        if turn >= 6 and tasks:
+            later(tasks.pop(0))
+            if tasks:
+                later(tasks.pop(0))
+    while tasks:
+        later(tasks.pop(0))
+    for _ in steps:
+        pass
+    note_waits(mail, notes_out, recv_n)
+    mail.finish()
+
+
+def moe(n2, g_all, cols, eg, ego, eu, euo, ed, edo, router, named, number):
+    shape, f32, low = jax.ShapeDtypeStruct, jnp.float32, jnp.bfloat16
+    vmem = pl.BlockSpec(memory_space=VMEM)
+    dma = pltpu.SemaphoreType.DMA
+    outs = (
+        shape((64, 1536), f32),
+        shape((16, 8, 128), f32),
+        shape((1024, 128), f32),
+        shape((1024, 1536), low),
+        shape((1536, 1280), f32),
+        shape((512, 1536), f32),
+        shape((1536, 128), f32),
+    )
+    return pl.pallas_call(
+        moe_kernel,
+        out_shape=outs,
+        in_specs=[vmem] * 11,
+        out_specs=(vmem,) * len(outs),
+        scratch_shapes=[
+            VMEM((1024, 1536), low),
+            VMEM((1024, 640), low),
+            VMEM((1024, 1280), low),
+            VMEM((16, 8, 128), f32),
+        ]
+        + reduce_scratch(64, 1536, low)
+        + [dma((42,)), dma((27,)), dma((16,))],
+        compiler_params=pltpu.CompilerParams(
+            collective_id=number, has_side_effects=True, vmem_limit_bytes=58 << 20
+        ),
+        name="moe",
+    )(n2, g_all, cols, eg, ego, eu, euo, ed, edo, router, named)
+
+
+def mix_backward_kernel(
+    dres_ref,
+    n1_ref,
+    cols_ref,
+    wbc_ref,
+    wdt_ref,
+    taps_ref,
+    head_ref,
+    gain_ref,
+    info_ref,
+    docrow_ref,
+    token_ref,
+    z_ref,
+    ext_ref,
+    pre_ref,
+    dt_ref,
+    y_ref,
+    state_ref,
+    moe_ref,
+    out_ref,
+    block_ref,
+    gmain_ref,
+    gbc_ref,
+    gdt_ref,
+    gtaps_ref,
+    gchan_ref,
+    ghead_ref,
+    part_ref,
+    dm_ref,
+    mixed_ref,
+    din_ref,
+    dpre_ref,
+    *refs,
+):
+    got, sums, refs = refs[:5], refs[5:8], refs[8:]
+    b_got, b_sums, refs = refs[:5], refs[5:8], refs[8:]
+    send, recv, b_send, b_recv = refs
+    here, side, z_at = peers()[:3]
+    greet(near(side))
+    low, f32 = jnp.bfloat16, jnp.float32
+    zs = layers(z_at)
+    b_mail = Mail(b_send)
+    b_steps = reduce_steps(b_mail, moe_ref, block_ref, b_got, b_sums, b_recv, 64)
+    next(b_steps)
+
+    @pl.loop(0, 4)
+    def _(i):
+        at = pl.ds(pl.multiple_of(i * LAYER, LAYER), LAYER)
+        dm_ref[at] = mm(dres_ref[at], cols_ref[:, 512:704])
+
+    next(b_steps)
+    rate, skip = head_ref[1:2], spread_heads(head_ref[2:3])
+    onehot = (
+        lax.broadcasted_iota(jnp.int32, (192, 128), 0) // HEADW
+        == lax.broadcasted_iota(jnp.int32, (192, 128), 1)
+    ).astype(f32)
+    row = lax.broadcasted_iota(jnp.int32, (CHUNK, CHUNK), 0)
+    lane = lanes((CHUNK, CHUNK))
+    above = (row <= lane).astype(f32)
+    lane192 = lanes((CHUNK, 192))
+    masks = [((lane192 // HEADW) == h).astype(f32) for h in range(3)]
+    d_state = jnp.zeros((128, 192), f32)
+    g_gain = jnp.zeros((1, 192), f32)
+    g_skip = jnp.zeros((1, 192), f32)
+    g_rate = jnp.zeros((1, 128), f32)
+    g_dt = jnp.zeros((1, 128), f32)
+    g_taps = [jnp.zeros((1, 448), f32) for _ in range(5)]
+    dpre_ref[1024:1032] = jnp.zeros((8, 448), f32)
+    for c in range(7, -1, -1):
+        r = c * CHUNK
+        at = pl.ds(r, CHUNK)
+        info, token = info_ref[at], token_ref[at]
+        scale, pull = token[:, 0:1], token[:, 1:2]
+        z, y, dm, gain = z_ref[at], y_ref[at], dm_ref[at], gain_ref[0:1]
+        sig = jax.nn.sigmoid(z)
+        gated = y * z * sig
+        scaled = gated * scale
+        mixed_ref[at] = (scaled * gain).astype(low)
+        g_gain = g_gain + jnp.sum(dm * scaled, axis=0, keepdims=True)
+        d_gated = scale * gain * dm - gated * pull
+        d_y = d_gated * z * sig
+        din_ref[at, 0:192] = (d_gated * y * silu_slope(z, sig)).astype(low)
+        pre = pre_ref[at]
+        pre_sig = jax.nn.sigmoid(pre)
+        act = pre * pre_sig
+        b, cc, x = act[:, 0:128], act[:, 128:256], act[:, 256:448]
+        g_skip = g_skip + jnp.sum(d_y * x, axis=0, keepdims=True)
+        dt = dt_ref[at]
+        step = soft_plus(dt)
+        logs, tables, step_t = chunk_tables(step, rate, info[:, 3:4], docrow_ref[0:1, at])
+        cross = mm_nt(cc, b)
+        decays = [tables[h] * step_t[h] for h in range(3)]
+        stacked = jnp.concatenate([cross * decays[h] for h in range(3)], 0)
+        d_ys = jnp.concatenate([d_y * masks[h] for h in range(3)], 0)
+        d_stack = mm_nt(d_ys, x)
+        d_x = skip * d_y + mm_tn(stacked, d_ys)
+        state = state_ref[c]
+        enters = jnp.exp(logs) * info[:, 4:5]
+        enters_x = spread_heads(enters)
+        d_in_y = enters_x * d_y
+        from_state = mm(cc, state)
+        tail_w = jnp.exp(logs[CHUNK - 1 :] - logs) * info[:, 5:6]
+        tail = tail_w * step
+        tail_x = spread_heads(tail)
+        to_state = mm(b, d_state)
+        d_x = d_x + tail_x * to_state
+        both = mm(
+            jnp.concatenate([d_y * from_state, x * to_state], 0), onehot, exact=True
+        )
+        d_enters, d_tail = both[:CHUNK], both[CHUNK:]
+        d_cross = jnp.zeros((CHUNK, CHUNK), f32)
+        row_sums = jnp.zeros((CHUNK, CHUNK), f32)
+        col_sums = []
+        for h in range(3):
+            d_a = d_stack[h * CHUNK : (h + 1) * CHUNK]
+            d_cross = d_cross + d_a * decays[h]
+            plain = d_a * cross * tables[h]
+            col_sums.append(jnp.sum(plain, axis=0, keepdims=True))
+            total = jnp.sum(plain * step_t[h], axis=1, keepdims=True)
+            row_sums = jnp.where(lane == h, total, row_sums)
+        col_sums = jnp.concatenate(col_sums + [jnp.zeros((5, CHUNK), f32)], 0)
+        col_sums = jnp.concatenate([col_sums, jnp.zeros((CHUNK - 8, CHUNK), f32)], 0).T
+        d_c = mm(d_cross, b) + mm_nt(d_in_y, state)
+        d_b = mm_tn(d_cross, cc) + mm_nt(tail_x * x, d_state)
+        kept = enters[CHUNK - 1 :]
+        d_kept = mm(
+            jnp.broadcast_to(jnp.sum(d_state * state, axis=0, keepdims=True), (8, 192)),
+            onehot,
+            exact=True,
+        )[0:1]
+        pulled = d_tail * tail
+        d_logs = row_sums - step * col_sums + d_enters * enters - pulled
+        d_last = jnp.sum(pulled, axis=0, keepdims=True) + d_kept * kept
+        d_logs = d_logs + jnp.where(row == CHUNK - 1, d_last, 0.0)
+        d_l = mm(above, d_logs, exact=True)
+        d_step = col_sums + d_tail * tail_w + d_l * rate
+        g_rate = g_rate + jnp.sum(d_l * step, axis=0, keepdims=True)
+        d_dt = jnp.where(lane < 3, d_step * jax.nn.sigmoid(dt), 0.0)
+        g_dt = g_dt + jnp.sum(d_dt, axis=0, keepdims=True)
+        din_ref[at, 768:896] = d_dt.astype(low)
+        d_state = spread_heads(kept) * d_state + mm_tn(cc, d_in_y)
+        d_pre = jnp.concatenate([d_b, d_c, d_x], 1) * silu_slope(pre, pre_sig)
+        dpre_ref[at] = d_pre
+        g_taps[4] = g_taps[4] + jnp.sum(d_pre, axis=0, keepdims=True)
+        g_taps[3] = g_taps[3] + jnp.sum(d_pre * ext_ref[pl.ds(r + 8, CHUNK)], axis=0, keepdims=True)
+        d_ext = taps_ref[3:4] * d_pre
+        for k in (1, 2, 3):
+            masked = d_pre * info[:, k - 1 : k]
+            g_taps[3 - k] = g_taps[3 - k] + jnp.sum(
+                masked * ext_ref[pl.ds(r + 8 - k, CHUNK)], axis=0, keepdims=True
+            )
+            after = pl.ds(r + k, CHUNK)
+            d_ext = d_ext + taps_ref[3 - k : 4 - k] * (
+                dpre_ref[after] * info_ref[after, k - 1 : k]
+            )
+        din_ref[at, 256:512] = d_ext[:, 0:256].astype(low)
+        din_ref[at, 512:704] = d_ext[:, 256:448].astype(low)
+        next(b_steps, None)
+    for k in range(5):
+        gtaps_ref[k : k + 1] = g_taps[k]
+    gchan_ref[0:1] = g_gain
+    gchan_ref[1:2] = g_skip
+    ghead_ref[0:1] = g_dt
+    ghead_ref[1:2] = g_rate * rate
+
+    def layer(k):
+        at = pl.ds(pl.multiple_of(zs[k] * LAYER, LAYER), LAYER)
+        total = mm_nt(din_ref[at, 0:192], cols_ref[:, 0:192])
+        total = total + mm_nt(din_ref[at, 256:512], wbc_ref[...])
+        total = total + mm_nt(din_ref[at, 512:704], cols_ref[:, 256:448])
+        total = total + mm_nt(din_ref[at, 768:896], wdt_ref[...])
+        part_ref[at] = total.astype(low)
+
+    def later(task):
+        if task == 0:
+            gmain_ref[:, 0:192] = mm_tn(n1_ref[...], din_ref[:, 0:192])
+        elif task == 1:
+            gmain_ref[:, 256:448] = mm_tn(n1_ref[...], din_ref[:, 512:704])
+        elif task == 2:
+            gmain_ref[:, 512:704] = mm_tn(dres_ref[...], mixed_ref[...])
+        elif task == 3:
+            gbc_ref[...] = mm_tn(n1_ref[...], din_ref[:, 256:512])
+        else:
+            gdt_ref[...] = mm_tn(n1_ref[...], din_ref[:, 768:896])
+
+    mail = Mail(send)
+    steps = reduce_steps(mail, part_ref, out_ref, got, sums, recv, 64)
+    left, tasks = [3, 2, 1, 0], [0, 1, 2, 3, 4]
+    for turn in range(13):
+        if turn in (0, 1, 3, 6):
+            layer(left.pop(0))
+        next(steps, None)
+        next(b_steps, None)
+        if turn >= 6 and tasks:
+            later(tasks.pop(0))
+    while tasks:
+        later(tasks.pop(0))
+    for _ in b_steps:
+        pass
+    for _ in steps:
+        pass
+    b_mail.finish()
+    mail.finish()
+
+
+def mix_backward(*args, number):
+    shape, f32, low = jax.ShapeDtypeStruct, jnp.float32, jnp.bfloat16
+    vmem = pl.BlockSpec(memory_space=VMEM)
+    dma = pltpu.SemaphoreType.DMA
+    outs = (
+        shape((64, 1536), f32),
+        shape((64, 1536), f32),
+        shape((1536, 768), f32),
+        shape((1536, 256), f32),
+        shape((1536, 128), f32),
+        shape((8, 448), f32),
+        shape((8, 192), f32),
+        shape((8, 128), f32),
+    )
+    return pl.pallas_call(
+        mix_backward_kernel,
+        out_shape=outs,
+        in_specs=[vmem] * len(args),
+        out_specs=(vmem,) * len(outs),
+        scratch_shapes=[
+            VMEM((1024, 1536), low),
+            VMEM((1024, 192), f32),
+            VMEM((1024, 192), low),
+            VMEM((1024, 896), low),
+            VMEM((1032, 448), f32),
+        ]
+        + reduce_scratch(64, 1536, low)
+        + reduce_scratch(64, 1536, low)
+        + [dma((27,)), dma((27,)), dma((27,)), dma((27,))],
+        compiler_params=pltpu.CompilerParams(
+            collective_id=number, has_side_effects=True, vmem_limit_bytes=60 << 20
+        ),
+        name="mix_backward",
+    )(*args)
 
 
 def by_heads(
@@ -1265,9 +1804,8 @@
     ids = jnp.concatenate([doc_ids[:, :, None], routes], 2)
     ids = lax.dynamic_index_in_dim(ids, side, 1, False)
     bc_half = lax.dynamic_slice_in_dim(w_bc, side * state, state, 1)
-    own_rows = jnp.concatenate(
+    own_extra = jnp.concatenate(
         [
-            n1_own,
             bc_half.reshape(8, width),
             router.reshape(1, width),
             padded(w_dt, 2),
@@ -1279,7 +1817,7 @@
     blocks = jnp.concatenate(
         [
             part.reshape(part.shape[0], 8, part.shape[1] // 8)
-            for part in (w_z, w_x, shared_gate, shared_up, w_out.T, shared_down.T)
+            for part in (w_z, shared_gate, w_x, shared_up, w_out.T, shared_down.T)
         ],
         2,
     ).transpose(1, 0, 2)
@@ -1294,13 +1832,11 @@
         0,
     )
     eg, eu, ed = expert_gate[0], expert_up[0], expert_down[0]
-    all_rows, extra_sib, cols, small_sib, eg_o, eu_o, ed_o = enter(
-        own_rows, blocks, small, eg, eu, ed, 1
-    )
-    all_rows = all_rows.reshape(places, 80, width)
+    n1, extra_own, extra_sib, cols, small_sib, eg_o, eu_o, ed_o = enter(
+        n1_own, own_extra, blocks, small, eg, eu, ed, 1
+    )
+    extra_own = extra_own.reshape(places, 16, width)
     extra_sib = extra_sib.reshape(places, 16, width)
-    n1 = all_rows[:, :block_len].reshape(length, width)
-    extra_own = all_rows[:, block_len:]
     wbc = ordered(
         extra_own[:, :8].reshape(width, state), extra_sib[:, :8].reshape(width, state), 1
     ).reshape(width, 2 * state)
@@ -1312,165 +1848,114 @@
     docs, picks = ids[:, 0], ids[:, 1:]
     small = mine_of(small, small_sib)
     wide_small = lax.dynamic_slice_in_dim(small, slot * chans, chans, 1)
-    taps = jnp.concatenate([wide_small[:KER], conv_bc], 1)
-    shift = jnp.concatenate([wide_small[KER], convb_bc], 0)
-    gn_gain = wide_small[KER + 1]
+    taps = jnp.concatenate(
+        [
+            jnp.concatenate([conv_bc, wide_small[:KER]], 1),
+            jnp.concatenate([convb_bc, wide_small[KER]], 0)[None],
+            jnp.zeros((3, 2 * state + chans), f32),
+        ],
+        0,
+    )
+    gn_gain = jnp.pad(wide_small[KER + 1][None], ((0, 7), (0, 0)))
     head_params = small[KER + 2, :72].reshape(3, 24)
     head_params = lax.dynamic_slice_in_dim(head_params, slot * heads, heads, 1)
-    bias_dt, rate_log, skip = head_params[0], head_params[1], head_params[2]
-    wz, wx, sg, su = cols[:, :192], cols[:, 192:384], cols[:, 384:448], cols[:, 448:512]
-    wout_t, sd_t = cols[:, 512:704], cols[:, 704:768]
+    head_params = jnp.stack([head_params[0], -jnp.exp(head_params[1]), head_params[2]])
+    head_params = jnp.pad(head_params, ((0, 5), (0, 128 - heads)))
+    wdt = jnp.pad(wdt, ((0, 0), (0, 128 - heads)))
+    wrouter = jnp.pad(wrouter, ((0, 0), (0, 128 - experts)))
+    docs_f = docs.astype(f32)
+    before = jnp.concatenate([jnp.full((KER - 1,), -1.0, f32), docs_f])
+    groups = docs_f.reshape(length // CHUNK, CHUNK)
+    ends = groups[:, -1]
+    starts = jnp.concatenate([docs_f[:1], ends[:-1]])
+    info = jnp.stack(
+        [(before[KER - 1 - k : KER - 1 - k + length] == docs_f).astype(f32) for k in (1, 2, 3)]
+        + [
+            docs_f,
+            (groups == starts[:, None]).astype(f32).reshape(-1),
+            (groups == ends[:, None]).astype(f32).reshape(-1),
+        ],
+        1,
+    )
+    info = jnp.pad(info, ((0, 8), (0, 128 - info.shape[1])))
+    docrow = jnp.broadcast_to(docs_f[None], (8, length))
+    named = jnp.sum((picks[:, :, None] == jnp.arange(128)).astype(f32), axis=1)
 
     def note(values):
         return jnp.pad(values.reshape(1, block_len), ((0, 7), (0, 128 - block_len)))
 
-    def notes(values):
-        return jnp.pad(
-            values.reshape(places, 1, block_len), ((0, 0), (0, 7), (0, 128 - block_len))
-        )
-
     def noted(array):
         return array[:, 0, :block_len]
 
-    win = jnp.concatenate([wz, wx, wbc, wdt], 1)
-    proj = flat_dot(n1, win)
-    gate_z = proj[:, :chans]
-    conv_in = proj[:, chans : 2 * chans + 2 * state]
-    dt_pre = proj[:, 2 * chans + 2 * state :] + bias_dt
-    conv_ext = jnp.concatenate([jnp.zeros((KER - 1, conv_in.shape[1]), jnp.float32), conv_in], 0)
-    docs_ext = jnp.concatenate([jnp.full((KER - 1,), -1, jnp.int32), docs], 0)
-
-    def local_conv(ext_part, weight_part, shift_part):
-        return conv_apply(ext_part, docs_ext, weight_part, shift_part)
-
-    conv_out, conv_back = jax.vjp(local_conv, conv_ext, taps, shift)
-    x_heads = conv_out[:, :chans].reshape(length, heads, head_size)
-    b_state = conv_out[:, chans : chans + state]
-    c_state = conv_out[:, chans + state :]
-    step_size = jax.nn.softplus(dt_pre)
-    decay_rate = -jnp.exp(rate_log)
-
-    def local_scan(x_part, step_part, b_part, c_part, rate_part):
-        return scan_core(x_part, step_part, b_part, c_part, rate_part, docs, 128)
-
-    core, scan_back = jax.vjp(local_scan, x_heads, step_size, b_state, c_state, decay_rate)
-    y_flat = (core + skip[:, None] * x_heads).reshape(length, chans)
-    gate_sig = jax.nn.sigmoid(gate_z)
-    gated = y_flat * gate_z * gate_sig
-    gained = (gated * gn_gain).astype(jnp.bfloat16)
-    out_part = flat_dot_t(gained, wout_t)
-    out_sum, squares = reduce_rows(out_part.astype(low), notes(jnp.sum(gated * gated, axis=-1)), 2)
+    weights = (cols, wbc, wdt, taps, head_params, gn_gain, info, docrow)
+    z, ext, pre, dt, y, states, out_sum, squares, g_all = mix_forward(n1, *weights, g_own, 2)
     scale_own = lax.rsqrt(jnp.sum(noted(squares), axis=0) / inner + EPS)[:, None]
     out_own = scale_own * out_sum
     residual = x_own + out_own
 
     scale_two = lax.rsqrt(jnp.mean(residual * residual, axis=-1, keepdims=True) + EPS)
-    n2_own = (residual * scale_two * norm2_gain).astype(jnp.bfloat16)
+    n2_own = (residual * scale_two * norm2_gain).astype(low)
     n2, scale_gated = gather_rows(n2_own, note(scale_own), 3)
-    scale_gated = noted(scale_gated).reshape(length, 1)
-    g_all, _ = gather_rows(g_own, note(scale_own), 4)
-    wup = jnp.concatenate([eg, eg_o, sg, eu, eu_o, su], 1)
-    wdown = jnp.concatenate([ed, ed_o, sd_t.T], 0)
-    wide = hidden + shared
-    logits = flat_dot(n2, wrouter)
-    named = jnp.sum((picks[:, :, None] == jnp.arange(experts)).astype(jnp.float32), axis=1)
-    top = jnp.max(jnp.where(named > 0, logits, -jnp.inf), axis=-1, keepdims=True)
-    raised = jnp.exp(jnp.where(named > 0, logits - top, 0.0)) * named
-    probs = raised / jnp.sum(raised, axis=-1, keepdims=True)
-    prob = lax.dynamic_slice_in_dim(probs, here, 1, 1)
-    col_prob = jnp.concatenate(
-        [jnp.broadcast_to(prob, (length, hidden)), jnp.ones((length, shared), jnp.float32)], 1
-    )
-    hid = flat_dot(n2, wup)
-    h_gate, h_up = hid[:, :wide], hid[:, wide:]
-    h_sig = jax.nn.sigmoid(h_gate)
-    act = h_gate * h_sig * h_up
-    act_low = (act * col_prob).astype(jnp.bfloat16)
-    moe_part = flat_dot(act_low, wdown)
-    block_sum, _ = reduce_rows(moe_part.astype(low), notes(jnp.zeros((length,), f32)), 5)
-    block_own = residual + block_sum
-
-    d_act = flat_dot_t(g_all, wdown)
-    prob_grad = jnp.sum((act * d_act)[:, :hidden], axis=-1)
-    d_act = d_act * col_prob
-    d_up = d_act * h_gate * h_sig
-    d_gate = d_act * h_up * silu_slope(h_gate, h_sig)
-    d_hid = jnp.concatenate([d_gate, d_up], 1).astype(jnp.bfloat16)
-    grad_down = outer_sum(act_low, g_all)
-    grad_up = outer_sum(n2, d_hid)
-    dn2_part = flat_dot_t(d_hid, wup)
-    dn2, prob_grads = reduce_rows(dn2_part.astype(low), notes(prob_grad), 6)
+    scale_gated = noted(scale_gated).reshape(length)
+    dn2, prob_grads, probs, moe_part, grad_up, grad_down, grad_sd = moe(
+        n2, g_all, cols, eg, eg_o, eu, eu_o, ed, ed_o, wrouter, named, 4
+    )
     prob_grads = noted(prob_grads).T
-    probs_own = lax.dynamic_slice_in_dim(probs, here * block_len, block_len, 0)
+    probs_own = lax.dynamic_slice(probs, (here * block_len, 0), (block_len, experts))
     d_logits = (
         probs_own * (prob_grads - jnp.sum(probs_own * prob_grads, axis=-1, keepdims=True))
-    ).astype(jnp.bfloat16)
+    ).astype(low)
     grad_router = outer_sum(n2_own, d_logits)
-    dn2 = dn2 + flat_dot_t(d_logits, wrouter)
+    dn2 = dn2 + flat_dot_t(d_logits, wrouter[:, :experts])
     d_norm, grad_norm2 = norm_back(dn2, residual, scale_two, norm2_gain)
-    d_res = g_own.astype(jnp.float32) + d_norm
-    d_res_low = d_res.astype(jnp.bfloat16)
-
-    cross_own = jnp.sum(d_res_low.astype(jnp.float32) * out_own, axis=-1, keepdims=True) / scale_own
-    d_res_all, cross = gather_rows(d_res_low, note(cross_own), 7)
-    cross = noted(cross).reshape(length, 1)
-    d_mixed = flat_dot(d_res_all, wout_t)
-    mixed_out = (gated * scale_gated * gn_gain).astype(jnp.bfloat16)
-    grad_out_t = outer_sum(d_res_all, mixed_out)
-    grad_gnorm = jnp.sum(d_mixed * gated * scale_gated, axis=0)
-    d_gated = scale_gated * gn_gain * d_mixed - gated * (
-        scale_gated * scale_gated * scale_gated * cross / inner
-    )
-    d_y = d_gated * gate_z * gate_sig
-    d_z = (d_gated * y_flat * silu_slope(gate_z, gate_sig)).astype(jnp.bfloat16)
-    d_y_heads = d_y.reshape(x_heads.shape)
-    grad_skip = jnp.sum(d_y_heads * x_heads, axis=(0, 2))
-    d_xh, d_step, d_b, d_c, d_rate = scan_back(d_y_heads)
-    d_xh = d_xh + skip[:, None] * d_y_heads
-    d_dt = d_step * jax.nn.sigmoid(dt_pre)
-    grad_dtb = jnp.sum(d_dt, axis=0)
-    grad_alog = d_rate * decay_rate
-    d_conv = jnp.concatenate([d_xh.reshape(length, chans), d_b, d_c], 1)
-    d_ext, grad_taps, grad_shift = conv_back(d_conv)
-    d_in = jnp.concatenate(
-        [d_z, d_ext[KER - 1 :].astype(jnp.bfloat16), d_dt.astype(jnp.bfloat16)], 1
-    )
-    grad_in = outer_sum(n1, d_in)
-    dn1, _ = reduce_rows(flat_dot_t(d_in, win).astype(low), notes(jnp.zeros((length,), f32)), 8)
+    d_res = g_own.astype(f32) + d_norm
+    d_res_low = d_res.astype(low)
+
+    cross_own = jnp.sum(d_res_low.astype(f32) * out_own, axis=-1, keepdims=True) / scale_own
+    d_res_all, cross = gather_rows(d_res_low, note(cross_own), 5)
+    cross = noted(cross).reshape(length)
+    pull = scale_gated * scale_gated * scale_gated * cross / inner
+    token = jnp.pad(jnp.stack([scale_gated, pull], 1), ((0, 0), (0, 126)))
+    dn1, block_sum, grad_main, grad_bc, grad_wdt, grad_taps, grad_chan, grad_head = mix_backward(
+        d_res_all, n1, *weights, token, z, ext, pre, dt, y, states, moe_part, number=6
+    )
+    block_own = residual + block_sum
     d_x, grad_norm1 = norm_back(dn1, x_own, scale_one, norm1_gain)
     input_own = d_res + d_x
 
     grads = jnp.concatenate(
         [
-            grad_in[:, : 2 * chans],
-            grad_up[:, hidden:wide],
-            grad_up[:, wide + hidden :],
-            grad_out_t,
-            grad_down[hidden:].T,
+            grad_main[:, :192],
+            grad_up[:, 576:640],
+            grad_main[:, 256:448],
+            grad_up[:, 1216:1280],
+            grad_main[:, 512:704],
+            grad_sd[:, 64:],
         ],
         1,
     ).astype(low)
     main = grads.reshape(places, 96, 768)
     bcr = jnp.concatenate(
         [
-            grad_in[:, 2 * chans : 2 * chans + 2 * state].reshape(places, 96, 256),
+            grad_bc.reshape(places, 96, 256),
             grad_router.reshape(places, 6, 256),
             jnp.zeros((places, 10, 256), f32),
         ],
         1,
     ).astype(low)
-    grad_wdt = grad_in[:, 2 * chans + 2 * state :]
+    grad_wdt = grad_wdt[:, :heads]
+    grad_skip = jnp.sum(grad_chan[1].reshape(heads, head_size), axis=1)
     singles = jnp.concatenate(
         [
             grad_norm1,
             grad_norm2,
-            grad_taps[:, chans:].reshape(-1),
-            grad_shift[chans:],
-            grad_taps[:, :chans].reshape(-1),
-            grad_shift[:chans],
-            grad_gnorm,
-            grad_dtb,
-            grad_alog,
+            grad_taps[:KER, : 2 * state].reshape(-1),
+            grad_taps[KER, : 2 * state],
+            grad_taps[:KER, 2 * state :].reshape(-1),
+            grad_taps[KER, 2 * state :],
+            grad_chan[0],
+            grad_head[0, :heads],
+            grad_head[1, :heads],
             grad_skip,
             grad_wdt.reshape(-1),
         ]
@@ -1496,7 +1981,7 @@
             block_own,
             input_own,
             grad_up[:, 256:512].astype(low),
-            grad_up[:, wide + 256 : wide + 512].astype(low),
+            grad_up[:, 896:1152].astype(low),
             grad_down[256:512].astype(low),
         ),
         10,
@@ -1506,7 +1991,7 @@
         ordered(input_own, other[1], 1),
         sums[0],
         joined(main[:, :, :192]),
-        joined(main[:, :, 192:384]),
+        joined(main[:, :, 256:448]),
         bc_sum,
         wdt_sum,
         joined(lists[0].reshape(8, KER, chans)),
@@ -1520,11 +2005,11 @@
         joined(main[:, :, 512:704]).T,
         sums[1],
         router_sum,
-        joined(main[:, :, 384:448]),
+        joined(main[:, :, 192:256]),
         joined(main[:, :, 448:512]),
         joined(main[:, :, 704:768]).T,
         (grad_up[:, :256] + other[2].astype(f32))[None],
-        (grad_up[:, wide : wide + 256] + other[3].astype(f32))[None],
+        (grad_up[:, 640:896] + other[3].astype(f32))[None],
         (grad_down[:256] + other[4].astype(f32))[None],
     )
 

time: 676 us -> 531 us (0.79)
  matrix products: 95.6 us -> 2.47 us
  local copies, waits for them, and re-layouts: 148 us -> 92.8 us
  Pallas kernels: 374 us -> 394 us
  other arithmetic: 47.6 us -> 31.4 us
    dot_general x17 -> x0, matrix products: 58.4 us -> none  [the longest x5 23.9 us: flat_dot(): jnp.dot(left_side.reshape(-1, left_side.shape[-1]), right_side, preferred...]
    pallas_call x5 -> x4, Pallas kernels: 187 us -> 245 us  [the longest x1 73.2 us: mix_forward(): pl.pallas_call(mix_forward_kernel, out_shape=outs, in_specs=[vmem] * 10,...]
    pallas_call x3 -> x2, Pallas kernels: 100 us -> 67.8 us  [gather_rows(): pl.pallas_call(functools.partial(gather_kernel, rows), out_shape=(jax.Sha...]
    dot_general x5 -> x1, matrix products: 19.1 us -> 1.45 us  [flat_dot_t(): lax.dot_general(left_side.reshape(-1, left_side.shape[-1]), right_side, (...]
    dot_general x5 -> x1, matrix products: 18.1 us -> 1.02 us  [outer_sum(): lax.dot_general(left_side.reshape(-1, left_side.shape[-1]), right_side.re...]
    pallas_call x1, Pallas kernels: 22.2 us -> 6.1 us  [swap(): pl.pallas_call(functools.partial(swap_kernel, count), out_shape=tuple((ja...]
    pallas_call x1, Pallas kernels: 64 us -> 75 us  [leave(): pl.pallas_call(leave_kernel, out_shape=(shape((8,) + main.shape[1:], low)...]
    slice x23 -> x13, local copies, waits for them, and re-layouts: 18.7 us -> 8.38 us  [the longest x2 1.38 us: by_heads(): starts = jnp.concatenate([docs_f[:1], ends[:-1]])]
where the time goes in v2:
time: 531 us; the launch traced here: 522 us
  Pallas kernels  394 us (74%)
  local copies, waits for them, and re-layouts  92.8 us (17%)
  other arithmetic  31.4 us (6%)
    pallas_call x1, Pallas kernels, leave(): pl.pallas_call(leave_kernel, out_shape=(shape((8,) + main.shape[1:], low)...  75 us
    pallas_call x1, Pallas kernels, mix_forward(): pl.pallas_call(mix_forward_kernel, out_shape=outs, in_specs=[vmem] * 10,...  73.2 us
    pallas_call x2, Pallas kernels, gather_rows(): pl.pallas_call(functools.partial(gather_kernel, rows), out_shape=(jax.Sha...  67.8 us
    pallas_call x1, Pallas kernels, enter(): pl.pallas_call(enter_kernel, out_shape=(shape((16 * rows, width), own.dty...  62.8 us
    pallas_call x1, Pallas kernels, mix_backward(): pl.pallas_call(mix_backward_kernel, out_shape=outs, in_specs=[vmem] * len...  60.1 us
    pallas_call x1, Pallas kernels, moe(): pl.pallas_call(moe_kernel, out_shape=outs, in_specs=[vmem] * 11, out_spec...  48.7 us
    unnamed x83, local copies, waits for them, and re-layouts  20.4 us

profile of v2, /device:TPU:15, one launch (start us, length us, event | category | flops | bytes accessed | tf_op | source)
XLA Modules:
  0.0 522.1 jit_solution(4125657999424782731)
XLA Ops:
  15.9 1.4 reshape.340
  17.4 3.3 concatenate.56
  20.7 62.8 %enter.1 = (bf16[1024,1536]{1,0:T(8,128)(2,1)}, bf16[256,1536]{1,0:T(8,128)(2,1)S(1)}, bf16[256,1536]{1,0:T(8,128)(2,1)S(1)}, bf16[1536,768]{1,0:T(8,128)(2,1)},...) custom-call(bf16[64,1536]{1,0:T(8,128)(2,1)S(1)} %fusion.3.own_ref, ...), custom_call_target="tpu_custom_call" | custom-call | tf_op jit(solution)/shard_map/enter/pallas_call | solution.py:901
  101.0 1.3 compare_convert_fusion
  104.5 2.4 convert_reduce_fusion.named_ref
  107.1 2.5 stack.73
  109.7 1.9 pad.54.info_ref
  111.5 73.2 %mix_forward.1 = (f32[1024,192]{1,0:T(8,128)}, f32[1032,448]{1,0:T(8,128)}, f32[1024,448]{1,0:T(8,128)}, f32[1024,128]{1,0:T(8,128)}, f32[1024,192]{1,0:T(8,128)...) custom-call(bf16[1024,1536]{1,0:T(8,128)(2,1)} %get-tuple-element.68.n1_ref,, ...), custom_call_target="tpu_custom_call" | custom-call | tf_op jit(solution)/shard_map/mix_forward/pallas_call | solution.py:1325
  187.0 35.3 %gather_3.1 = (bf16[1024,1536]{1,0:T(8,128)(2,1)S(1)}, f32[16,8,128]{2,1,0:T(8,128)S(1)}) custom-call(bf16[64,1536]{1,0:T(8,128)(2,1)S(1)} %multiply_convert_fusion.own_ref, f32[8,128]{1,0:T(8,128)S(1)} %pad.55.note_ref), custom_call_target="tpu_custom_call" | custom-call | tf_op jit(solution)/shard_map/gather_3/pallas_call | solution.py:652
  222.4 1.6 copy-done.3
  224.0 48.7 %moe.1 = (f32[64,1536]{1,0:T(8,128)}, f32[16,8,128]{2,1,0:T(8,128)}, f32[1024,128]{1,0:T(8,128)}, bf16[1024,1536]{1,0:T(8,128)(2,1)}, f32[1536,1280]{1,0:T(8,128...) custom-call(bf16[1024,1536]{1,0:T(8,128)(2,1)} %copy-done.3, bf16[1024,1536]{1,0:T(8,128)(2,1)} %get-tuple-element.76.g_ref, ...), custom_call_target="tpu_custom_call" | custom-call | tf_op jit(solution)/shard_map/moe/pallas_call | solution.py:1481
  272.7 1.4 slice.340
  276.0 1.4 multiply_reduce_fusion
  279.5 2.4 slice.339.refs_4_
  281.9 32.5 %gather_5.1 = (bf16[1024,1536]{1,0:T(8,128)(2,1)S(1)}, f32[16,8,128]{2,1,0:T(8,128)S(1)}) custom-call(bf16[64,1536]{1,0:T(8,128)(2,1)S(1)} %get-tuple-element.237.own_ref, f32[8,128]{1,0:T(8,128)S(1)} %pad.57.note_ref), custom_call_target="tpu_custom_call" | custom-call | tf_op jit(solution)/shard_map/gather_5/pallas_call | solution.py:652
  314.4 1.6 copy-done.2
  317.3 60.1 %mix_backward.1 = (f32[64,1536]{1,0:T(8,128)}, f32[64,1536]{1,0:T(8,128)}, f32[1536,768]{1,0:T(8,128)}, f32[1536,256]{1,0:T(8,128)}, f32[1536,128]{1,0:T(8,128)}...) custom-call(bf16[1024,1536]{1,0:T(8,128)(2,1)} %copy-done.2, bf16[1024,1536]{1,0:T(8,128)(2,1)} %get-tuple-element.68.n1_ref, ...), custom_call_target="tpu_custom_call" | custom-call | tf_op jit(solution)/shard_map/mix_backward/pallas_call | solution.py:1720
  377.4 1.9 add.131.refs_0_
  385.2 1.9 fusion.6.refs_1_
  387.1 1.6 reshape.350
  390.7 2.8 convert.46
  397.3 4.7 concatenate.70.main_ref
  402.1 75.0 %leave.1 = (bf16[8,96,768]{2,1,0:T(8,128)(2,1)}, f32[112,256]{1,0:T(8,128)}, f32[16,88,128]{2,1,0:T(8,128)}) custom-call(bf16[16,96,768]{2,1,0:T(8,128)(2,1)} %concatenate.70.main_ref, bf16[16,112,256]{2,1,0:T(8,128)(2,1)} %maximum_maximum_fusion.bcr_ref, f32[88,128]{1,0:T(8,128)} %pad_bitcast_fusion.small_ref), custom_call_target="tpu_custom_call" | custom-call | tf_op jit(solution)/shard_map/leave/pallas_call | solution.py:1082
  479.0 1.5 slice.250
  487.4 6.1 %swap_10.1 = (f32[64,1536]{1,0:T(8,128)}, f32[64,1536]{1,0:T(8,128)}, bf16[1536,256]{1,0:T(8,128)(2,1)}, bf16[1536,256]{1,0:T(8,128)(2,1)}, bf16[256,1536]{1,0:T(8,128)(2,1)}) custom-call(f32[64,1536]{1,0:T(8,128)} %add.131.refs_0_, f32[64,1536]{1,0:T(8,128)} %fusion.6.refs_1_, bf16[1536,256]{1,0:T(8,128)(2,1)} %get-tuple-element.248.refs_2_, ...), custom_call_target="tpu_custom_call" | custom-call | tf_op jit(solution)/shard_map/swap_10/pallas_call | solution.py:1131
  493.5 2.6 add_bitcast_fusion
  496.1 4.0 add_bitcast_fusion.1
  500.2 1.5 copy.227
  501.7 1.5 copy.228
  503.2 2.1 copy.220
  505.3 3.5 reshape.355
  510.8 1.5 convert_element_type.127
  (235 shorter events, 74.3 us)
Async XLA Ops:
  0.7 11.8 %copy-start = (bf16[64,2,1536]{2,1,0:T(2,128)(2,1)S(1)}, bf16[64,2,1536]{2,1,0:T(2,128)(2,1)}, u32[]{:S(2)}) copy-start(bf16[64,2,1536]{2,1,0:T(2,128)(2,1)} %param.51) | copy-start | bytes 1179652
  0.7 13.0 %copy-start.22 = (bf16[64,2,1536]{2,1,0:T(2,128)(2,1)S(1)}, bf16[64,2,1536]{2,1,0:T(2,128)(2,1)}, u32[]{:S(2)}) copy-start(bf16[64,2,1536]{2,1,0:T(2,128)(2,1)} %param.26) | copy-start | bytes 1179652
  5.7 8.5 %copy-start.28 = (f32[1536]{0:T(1024)S(1)}, f32[1536]{0:T(1024)}, u32[]{:S(2)}) copy-start(f32[1536]{0:T(1024)} %param.29) | copy-start | bytes 18436
  8.6 5.7 %copy-start.25 = (bf16[96,1536]{1,0:T(8,128)(2,1)S(1)}, bf16[96,1536]{1,0:T(8,128)(2,1)}, u32[]{:S(2)}) copy-start(bf16[96,1536]{1,0:T(8,128)(2,1)} %param.30) | copy-start | bytes 884740
  12.5 2.3 copy-start.26
  12.9 3.0 copy-start.13
  14.2 3.2 copy-start.9
  15.9 4.8 copy-start.4
  15.9 4.8 copy-start.5
  20.7 65.7 %copy-start.30 = (f32[256]{0:T(256)S(1)}, f32[256]{0:T(256)}, u32[]{:S(2)}) copy-start(f32[256]{0:T(256)} %param.37) | copy-start | bytes 3076
  20.7 67.1 %copy-start.29 = (f32[4,256]{1,0:T(4,128)S(1)}, f32[4,256]{1,0:T(4,128)}, u32[]{:S(2)}) copy-start(f32[4,256]{1,0:T(4,128)} %param.35) | copy-start | bytes 12292
  83.6 0.9 copy-start.6
  84.4 0.9 copy-start.7
  111.5 74.1 %copy-start.10 = (bf16[64,1536]{1,0:T(8,128)(2,1)S(1)}, bf16[64,1536]{1,0:T(8,128)(2,1)}, u32[]{:S(2)}) copy-start(bf16[64,1536]{1,0:T(8,128)(2,1)} %copy-done.9) | copy-start | bytes 589828
  111.5 75.4 %copy-start.27 = (f32[1536]{0:T(1024)S(1)}, f32[1536]{0:T(1024)}, u32[]{:S(2)}) copy-start(f32[1536]{0:T(1024)} %param.43) | copy-start | bytes 18436
  222.4 1.7 copy-start.3
  272.7 5.8 %copy-start.14 = (bf16[64,1,1536]{2,1,0:T(2,128)(2,1)S(1)}, bf16[64,1,1536]{2,1,0:T(2,128)(2,1)}, u32[]{:S(2)}) copy-start(bf16[64,1,1536]{2,1,0:T(2,128)(2,1)} %copy-done.13) | copy-start | bytes 589828
  272.7 5.8 %copy-start.19 = (f32[64,1536]{1,0:T(8,128)S(1)}, f32[64,1536]{1,0:T(8,128)}, u32[]{:S(2)}) copy-start(f32[64,1536]{1,0:T(8,128)} %get-tuple-element.74) | copy-start | bytes 1179652
  314.4 1.7 copy-start.2
  377.4 12.0 %copy-start.17 = (f32[1536,256]{1,0:T(8,128)S(1)}, f32[1536,256]{1,0:T(8,128)}, u32[]{:S(2)}) copy-start(f32[1536,256]{1,0:T(8,128)} %get-tuple-element.101) | copy-start | bytes 4718596
  389.4 4.3 slice-start
  390.7 4.0 slice-start.1
  485.8 7.7 %copy-start.16 = (f32[512,1536]{1,0:T(8,128)S(1)}, f32[512,1536]{1,0:T(8,128)}, u32[]{:S(2)}) copy-start(f32[512,1536]{1,0:T(8,128)} %get-tuple-element.96) | copy-start | bytes 9437188
  493.5 2.6 copy-start.20
  493.5 2.6 copy-start.21
  496.1 4.0 copy-start.11
  496.1 4.0 copy-start.24
  500.1 1.6 copy-start.12
  500.1 1.6 copy-start.23
  515.4 1.5 copy-start.18
  515.4 3.5 copy-start.15
  518.8 3.1 copy-start.1
  (1 other events, 0.9 us)
